TPU v7x, 1024 devices: a whole 8x8x8 slice. The times are simulated.
1024 devices in a mesh: rep: 16 (over z, core), node: 8 (over x), local: 8 (over y).
Axes of the slice: x: 8, y: 8, z: 8, core: 2. Of those that a mesh axis runs over, the one named last changes fastest.
Arguments:
- tokens: bfloat16 [4096, 3584], P(('node', 'local'), 'rep'), may hold values from -6 to 6
- expert_ids: int32 [4096, 4], P(('node', 'local')), may hold values from 0 to 63, as said below
- route_weights: bfloat16 [4096, 4], P(('node', 'local')), may hold values from 0.099609375 to 0.5
- w_gate: bfloat16 [64, 3584, 1024], P(('node', 'local'), 'rep'), may hold values from -0.09375 to 0.09375
- w_up: bfloat16 [64, 3584, 1024], P(('node', 'local'), 'rep'), may hold values from -0.09375 to 0.09375
- w_down: bfloat16 [64, 1024, 3584], P(('node', 'local'), None, 'rep'), may hold values from -0.1875 to 0.1875
- grad_out: bfloat16 [4096, 3584], P(('node', 'local'), 'rep'), may hold values from -6 to 6
Outputs:
- mixed: bfloat16 [4096, 3584], P(('node', 'local'), 'rep')
- token_grad: bfloat16 [4096, 3584], P(('node', 'local'), 'rep')
- gate_weight_grad: bfloat16 [64, 3584, 1024], P(('node', 'local'), 'rep')
- up_weight_grad: bfloat16 [64, 3584, 1024], P(('node', 'local'), 'rep')
- down_weight_grad: bfloat16 [64, 1024, 3584], P(('node', 'local'), None, 'rep')
Inputs may be any that keep to these rules, and one draw needn't show every extreme that they name: `expert_ids`: each token names 4 different experts; picks 0 and 1 lie in one node group and picks 2 and 3 in another (expert e lies in group e // 8). The 64 tokens of one device visit every node group exactly 16 times. The tokens of one device name each expert at most 6 times, and in every draw some expert is named exactly 6 times by the tokens of every device.
All inputs are finite; a program needn't handle non-finite values.
Results may differ from a plain program's by a relative error of at most 0.0072.
Values may be sent and summed in bfloat16 or wider, within the bound.
No kernel may reach another device: no remote copies, remote signals or barrier semaphores. Data moves between devices by JAX's collectives and lax.ppermute only.
A program may use at most 32 MiB of HBM per device.

v0:
```python
import jax
import jax.numpy as jnp
from jax import lax
from jax.sharding import PartitionSpec as P


def silu_grads(gate_val, up_val, hidden_grad):
    sigmoid_val = jax.nn.sigmoid(gate_val)
    gate_grad = hidden_grad * up_val * (sigmoid_val * (1.0 + gate_val * (1.0 - sigmoid_val)))
    up_grad = hidden_grad * (gate_val * sigmoid_val)
    return (gate_grad.astype(jnp.bfloat16), up_grad.astype(jnp.bfloat16))


def gather_rows(table, index):
    return jnp.take(table, index, axis=0)


def earlier_counts(flat_ids, count):
    labels = jnp.arange(count, dtype=jnp.int32)
    onehot = (flat_ids[:, None] == labels[None, :]).astype(jnp.int32)
    before = jnp.cumsum(onehot, axis=0) - onehot
    return jnp.sum(before * onehot, axis=1)


def by_columns(token_rows, grad_rows, gate_mat, up_mat, down_mat):
    contract_cross = (((0,), (1,)), ((), ()))
    contract_first = (((0,), (0,)), ((), ()))
    contract_last = (((1,), (1,)), ((), ()))
    gate_cols = gate_mat
    up_cols = up_mat
    gate_up = lax.psum_scatter(
        jnp.stack(
            [
                lax.dot_general(
                    gate_cols, token_rows, contract_cross, preferred_element_type=jnp.float32
                ),
                lax.dot_general(
                    up_cols, token_rows, contract_cross, preferred_element_type=jnp.float32
                ),
            ],
            axis=1,
        ),
        "rep",
        scatter_dimension=0,
        tiled=True,
    )
    gate_val = gate_up[:, 0]
    up_val = gate_up[:, 1]
    hidden = (jax.nn.silu(gate_val) * up_val).astype(jnp.bfloat16)
    piece = lax.all_gather(hidden, "rep", axis=0, tiled=True)
    down_rows = down_mat
    outputs = lax.dot_general(piece, down_rows, contract_first, preferred_element_type=jnp.float32)
    down_sum = jnp.dot(piece, grad_rows, preferred_element_type=jnp.float32)
    outputs, down_sum = (outputs, down_sum)
    down_rows = down_mat
    hidden_grad = lax.psum_scatter(
        lax.dot_general(down_rows, grad_rows, contract_last, preferred_element_type=jnp.float32),
        "rep",
        scatter_dimension=0,
        tiled=True,
    )
    gate_grad, up_grad = silu_grads(gate_val, up_val, hidden_grad)
    piece = lax.all_gather(jnp.stack([gate_grad, up_grad], axis=1), "rep", axis=0, tiled=True)
    gate_cols = gate_mat
    up_cols = up_mat
    portion = lax.dot_general(
        piece[:, 0], gate_cols, contract_cross, preferred_element_type=jnp.float32
    )
    portion = portion + lax.dot_general(
        piece[:, 1], up_cols, contract_cross, preferred_element_type=jnp.float32
    )
    input_grad = portion
    gate_sum = lax.dot_general(
        token_rows, piece[:, 0], contract_cross, preferred_element_type=jnp.float32
    )
    up_sum = lax.dot_general(
        token_rows, piece[:, 1], contract_cross, preferred_element_type=jnp.float32
    )
    input_grad, gate_sum, up_sum = (input_grad, gate_sum, up_sum)
    return (
        outputs.astype(jnp.bfloat16),
        input_grad.astype(jnp.bfloat16),
        gate_sum.astype(jnp.bfloat16),
        up_sum.astype(jnp.bfloat16),
        down_sum.astype(jnp.bfloat16),
    )


def expert_work(token_rows, grad_rows, w_gate, w_up, w_down):
    results = by_columns(token_rows, grad_rows, w_gate[0], w_up[0], w_down[0])
    return results


def shards(tokens, expert_ids, route_weights, w_gate, w_up, w_down, grad_out):
    tok_count, width = tokens.shape
    picks = expert_ids.shape[1]
    node_count = lax.axis_size("node")
    local_count = lax.axis_size("local")
    experts = node_count * local_count
    node_hits = 2 * tok_count // node_count
    mean_count = 2 * node_hits // local_count
    depth = min(mean_count + max(mean_count // 2, 1), node_hits)
    weights = route_weights.astype(jnp.float32)
    flat_ids = expert_ids.reshape(-1)
    pick_row = flat_ids * depth + earlier_counts(flat_ids, experts)
    buffer_slots = jnp.arange(experts * depth, dtype=jnp.int32)
    buffer_hits = buffer_slots[:, None] == pick_row[None, :]
    placed = jnp.sum(
        buffer_hits.astype(jnp.float32).reshape(experts * depth, tok_count, picks), axis=2
    ).astype(jnp.bfloat16)
    row_weight = jnp.sum(jnp.where(buffer_hits, weights.reshape(-1)[None, :], 0.0), axis=1)
    send_tokens = (
        jnp.dot(placed, tokens, preferred_element_type=jnp.float32)
        .astype(jnp.bfloat16)
        .reshape(experts, depth, width)
    )
    send_grads = (
        (jnp.dot(placed, grad_out, preferred_element_type=jnp.float32) * row_weight[:, None])
        .astype(jnp.bfloat16)
        .reshape(experts, depth, width)
    )
    arrived, arrived_grads = (
        lax.all_to_all(send_tokens, ("node", "local"), split_axis=0, concat_axis=0, tiled=True),
        lax.all_to_all(send_grads, ("node", "local"), split_axis=0, concat_axis=0, tiled=True),
    )
    outputs, input_grad, gate_sum, up_sum, down_sum = expert_work(
        arrived.reshape(-1, width), arrived_grads.reshape(-1, width), w_gate, w_up, w_down
    )
    back_out, back_in = (
        lax.all_to_all(
            outputs.reshape(experts, depth, width),
            ("node", "local"),
            split_axis=0,
            concat_axis=0,
            tiled=True,
        ),
        lax.all_to_all(
            input_grad.reshape(experts, depth, width),
            ("node", "local"),
            split_axis=0,
            concat_axis=0,
            tiled=True,
        ),
    )
    picked_out = (
        gather_rows(back_out.reshape(-1, width), pick_row)
        .reshape(tok_count, picks, width)
        .astype(jnp.float32)
        * weights[:, :, None]
    )
    picked_in = (
        gather_rows(back_in.reshape(-1, width), pick_row)
        .reshape(tok_count, picks, width)
        .astype(jnp.float32)
    )
    part_out = lax.optimization_barrier(
        (picked_out[:, 0::2] + picked_out[:, 1::2]).astype(jnp.bfloat16)
    ).astype(jnp.float32)
    part_in = lax.optimization_barrier(
        (picked_in[:, 0::2] + picked_in[:, 1::2]).astype(jnp.bfloat16)
    ).astype(jnp.float32)
    mixed = (part_out[:, 0] + part_out[:, 1]).astype(jnp.bfloat16)
    token_grad = (part_in[:, 0] + part_in[:, 1]).astype(jnp.bfloat16)
    return (mixed, token_grad, gate_sum[None], up_sum[None], down_sum[None])


def solution(mesh):
    return jax.shard_map(
        shards,
        mesh=mesh,
        in_specs=(
            P(("node", "local"), "rep"),
            P(("node", "local"), None),
            P(("node", "local"), None),
            P(("node", "local"), "rep", None),
            P(("node", "local"), "rep", None),
            P(("node", "local"), None, "rep"),
            P(("node", "local"), "rep"),
        ),
        out_specs=(
            P(("node", "local"), "rep"),
            P(("node", "local"), "rep"),
            P(("node", "local"), "rep", None),
            P(("node", "local"), "rep", None),
            P(("node", "local"), None, "rep"),
        ),
        check_vma=False,
    )
```

profile of v0, /device:TPU:16, one launch (start us, length us, event | category | flops | bytes accessed | tf_op | source)
XLA Modules:
  0.0 343.3 jit_solution(3084406801443904387)
XLA Ops:
  7.2 0.9 copy.93
  8.3 0.6 reduce-window.6
  8.9 0.2 slice_reduce_fusion
  9.5 0.7 multiply_add_fusion
  10.3 1.0 convolution_convert_fusion.4
  11.3 0.1 copy.97
  11.5 29.3 %all_to_all.20 = bf16[64,6,224]{2,1,0:T(8,128)(2,1)S(1)} all-to-all(bf16[64,6,224]{2,1,0:T(8,128)(2,1)S(1)} %reshape.89), channel_id=1, replica_groups=mesh['rep'=16,'node'=8,'local'=8] {'node','local'}, dimensions={0} | all-to-all | bytes 344064 | tf_op jit(solution)/shard_map/all_to_all | solution.py:123
  41.0 0.4 convolution_bitcast_fusion.1
  41.4 0.4 convolution_bitcast_fusion.2
  41.7 1.9 pad_maximum_fusion
  43.6 5.9 %copy.98 = f32[1024,2,384]{2,1,0:T(2,128)} copy(f32[1024,2,384]{0,2,1:T(8,128)} %pad_maximum_fusion) | data formatting | bytes 6291456 | tf_op jit(solution)/shard_map/stack | solution.py:32
  49.6 0.6 copy-done.7
  50.4 0.5 copy-done.4
  50.9 0.1 select_reduce_fusion
  51.0 0.3 fusion.3
  51.3 0.1 copy.103
  51.5 17.3 %all_to_all.21 = bf16[64,6,224]{2,1,0:T(8,128)(2,1)S(1)} all-to-all(bf16[64,6,224]{2,1,0:T(8,128)(2,1)S(1)} %reshape.93), channel_id=1, replica_groups=mesh['rep'=16,'node'=8,'local'=8] {'node','local'}, dimensions={0} | all-to-all | bytes 344064 | tf_op jit(solution)/shard_map/all_to_all | solution.py:124
  69.0 0.4 convolution_bitcast_fusion
  69.3 1.6 copy.110
  71.0 1.3 dynamic-slice
  73.0 109.0 %all-reduce.3.cloned.1.call-done = f32[1024,2,384]{2,1,0:T(2,128)} async-done(((f32[1024,2,384]{2,1,0:T(2,128)}), f32[1024,2,384]{2,1,0:T(2,128)}) %all-reduce.3.cloned.1.call-update) | async-done | bytes 3145744
  182.0 1.2 constant_dynamic-slice_fusion
  183.2 66.5 %reduce-scatter.4.cloned.1.call-done = f32[64,384]{1,0:T(8,128)} async-done(((f32[1024,384]{1,0:T(8,128)}), f32[64,384]{1,0:T(8,128)}) %reduce-scatter.4.cloned.1.call-update) | async-done | bytes 98320 | tf_op jit(solution)/shard_map/reduce_scatter | solution.py:56
  249.7 1.0 fusion.23
  250.7 0.7 copy.106
  251.4 16.6 %all_gather.6 = bf16[1024,384]{1,0:T(8,128)(2,1)S(1)} all-gather(bf16[64,384]{1,0:T(8,128)(2,1)S(1)} %get-tuple-element.14), channel_id=1, replica_groups=mesh['rep'=16,'node'=8,'local'=8] {'rep'}, dimensions={0}, use_global_device_ids=true | all-gather | bytes 835584 | tf_op jit(solution)/shard_map/all_gather | solution.py:50
  268.1 0.4 convolution_convert_fusion.3
  268.6 0.8 reshape.91
  269.4 12.7 %all-to-all-start.1 = ((bf16[64,6,224]{2,1,0:T(8,128)(2,1)}), bf16[64,6,224]{2,1,0:T(8,128)(2,1)S(1)}, u32[]{:S(2)}, u32[]{:S(2)}) async-start(bf16[64,6,224]{2,1,0:T(8,128)(2,1)} %reshape.91), calls=%async_computation.1 | async-start | bytes 524288 | tf_op jit(solution)/shard_map/all_to_all | solution.py:130
  282.2 1.2 fusion.2
  283.4 13.4 %all-to-all-done.1 = bf16[64,6,224]{2,1,0:T(8,128)(2,1)S(1)} async-done(((bf16[64,6,224]{2,1,0:T(8,128)(2,1)}), bf16[64,6,224]{2,1,0:T(8,128)(2,1)S(1)}, u32[]{:S(2)}, u32[]{:S(2)}) %all-to-all-start.1) | async-done | bytes 172064 | tf_op jit(solution)/shard_map/all_to_all | solution.py:130
  296.9 1.2 gather_fusion
  298.1 4.4 %fusion.26 = (bf16[1024,1,384]{2,1,0:T(2,128)(2,1)S(1)}, bf16[1024,1,384]{2,1,0:T(2,128)(2,1)S(1)}) fusion(bf16[1024,2,384]{2,1,0:T(2,128)(2,1)} %all-gather.2.cloned.1.call-done), kind=kLoop, calls=%fused_computation.72 | loop fusion | bytes 3145728 | tf_op jit(solution)/shard_map/slice | solution.py:70
  302.6 1.2 copy-done.1
  303.7 0.4 fusion.9
  304.1 0.4 fusion.4
  304.5 0.1 copy.109
  304.7 0.8 reshape.95
  305.5 11.5 %all-to-all-start.3 = ((bf16[64,6,224]{2,1,0:T(8,128)(2,1)}), bf16[64,6,224]{2,1,0:T(8,128)(2,1)S(1)}, u32[]{:S(2)}, u32[]{:S(2)}) async-start(bf16[64,6,224]{2,1,0:T(8,128)(2,1)} %reshape.95), calls=%async_computation.3 | async-start | bytes 524288 | tf_op jit(solution)/shard_map/all_to_all | solution.py:137
  317.0 2.7 fusion
  319.6 1.2 fusion.1
  320.9 10.7 %all-to-all-done.3 = bf16[64,6,224]{2,1,0:T(8,128)(2,1)S(1)} async-done(((bf16[64,6,224]{2,1,0:T(8,128)(2,1)}), bf16[64,6,224]{2,1,0:T(8,128)(2,1)S(1)}, u32[]{:S(2)}, u32[]{:S(2)}) %all-to-all-start.3) | async-done | bytes 172064 | tf_op jit(solution)/shard_map/all_to_all | solution.py:137
  331.7 1.2 gather_fusion.1
  333.2 0.6 slice.48
  333.8 0.6 slice.49
  334.5 0.6 slice.54
  335.1 0.6 slice.55
  336.2 0.6 copy_bitcast_fusion.7
  (52 shorter events, 2.7 us)
Async XLA Ops:
  7.2 61.8 %copy-start = (bf16[1,1024,224]{1,2,0:T(8,128)(2,1)S(1)}, bf16[1,1024,224]{1,2,0:T(8,128)(2,1)}, u32[]{:S(2)}) copy-start(bf16[1,1024,224]{1,2,0:T(8,128)(2,1)} %param.14) | copy-start | bytes 1376260
  7.2 33.8 %copy-start.3 = (bf16[1,224,1024]{2,1,0:T(8,128)(2,1)S(1)}, bf16[1,224,1024]{2,1,0:T(8,128)(2,1)}, u32[]{:S(2)}) copy-start(bf16[1,224,1024]{2,1,0:T(8,128)(2,1)} %param.13) | copy-start | bytes 1376260
  7.2 174.8 %all-reduce.3.cloned.1.call-start = ((), (), s32[]{:S(2)}) async-start(), calls=%async_computation.7 | async-start | bytes 6291456
  11.5 29.8 %copy-start.2 = (bf16[1,224,1024]{2,1,0:T(8,128)(2,1)S(1)}, bf16[1,224,1024]{2,1,0:T(8,128)(2,1)}, u32[]{:S(2)}) copy-start(bf16[1,224,1024]{2,1,0:T(8,128)(2,1)} %param.12) | copy-start | bytes 1376260
  49.5 0.7 copy-start.7
  49.5 1.5 copy-start.6
  49.5 200.2 %reduce-scatter.4.cloned.1.call-start = ((), (), s32[]{:S(2)}) async-start(), calls=%async_computation.6 | async-start | bytes 1671168 | tf_op jit(solution)/shard_map/reduce_scatter | solution.py:56
  50.3 0.6 copy-start.4
  71.0 227.1 %all-gather.2.cloned.1.call-start = ((), (), s32[]{:S(2)}) async-start(), calls=%async_computation.5 | async-start | bytes 1671168 | tf_op jit(solution)/shard_map/all_gather | solution.py:63
  269.4 27.4 %all-to-all-start.1 = ((bf16[64,6,224]{2,1,0:T(8,128)(2,1)}), bf16[64,6,224]{2,1,0:T(8,128)(2,1)S(1)}, u32[]{:S(2)}, u32[]{:S(2)}) async-start(bf16[64,6,224]{2,1,0:T(8,128)(2,1)} %reshape.91), calls=%async_computation.1 | async-start | bytes 524288 | tf_op jit(solution)/shard_map/all_to_all | solution.py:130
  302.5 1.2 copy-start.1
  305.5 26.1 %all-to-all-start.3 = ((bf16[64,6,224]{2,1,0:T(8,128)(2,1)}), bf16[64,6,224]{2,1,0:T(8,128)(2,1)S(1)}, u32[]{:S(2)}, u32[]{:S(2)}) async-start(bf16[64,6,224]{2,1,0:T(8,128)(2,1)} %reshape.95), calls=%async_computation.3 | async-start | bytes 524288 | tf_op jit(solution)/shard_map/all_to_all | solution.py:137
  320.9 12.1 %copy-start.5 = (f32[64,4]{1,0:T(8,128)S(1)}, f32[64,4]{1,0:T(8,128)}, u32[]{:S(2)}) copy-start(f32[64,4]{1,0:T(8,128)} %copy-done.4) | copy-start | bytes 3076
Sparse Core Ops, SparseCore 0:
  49.6 132.3 all-reduce.2
  185.4 64.2 reduce-scatter.3
  253.3 43.4 all-gather.1
where the time goes:
time: 344 us; the launch traced here: 343 us
  waiting for transfers between devices  200 us (58%)
  blocking collectives  63.2 us (18%)
  local copies, waits for them, and re-layouts  27.4 us (8%)
  starting transfers between devices  24.4 us (7%)
  between operations  14.8 us (4%)
  matrix products  8.7 us (3%)
  other arithmetic  5.21 us (2%)
    unnamed x4, waiting for transfers between devices  109 us
    reduce_scatter x1, waiting for transfers between devices, by_columns(): lax.psum_scatter(lax.dot_general(down_rows, grad_rows, contract_last, pre...  66.5 us
    all_to_all x1, blocking collectives, shards(): lax.all_to_all(send_tokens, ('node', 'local'), split_axis=0, concat_axis=...  29.3 us
    all_to_all x1, blocking collectives, shards(): lax.all_to_all(send_grads, ('node', 'local'), split_axis=0, concat_axis=0...  17.3 us
    all_gather x1, blocking collectives, by_columns(): piece = lax.all_gather(hidden, 'rep', axis=0, tiled=True)  16.6 us
    all_to_all x1, waiting for transfers between devices, shards(): lax.all_to_all(outputs.reshape(experts, depth, width), ('node', 'local'),...  13.4 us
    all_to_all x1, starting transfers between devices, shards(): lax.all_to_all(outputs.reshape(experts, depth, width), ('node', 'local'),...  12.7 us
    all_to_all x1, starting transfers between devices, shards(): lax.all_to_all(input_grad.reshape(experts, depth, width), ('node', 'local...  11.5 us
  transfers between devices with their start and end apart: 5, of which 4 were waited for; matrix products, arithmetic and copies ran while one was open for 4% of the time, Pallas kernels for 0%

commit v1 on v0

v1 whole, which is shorter than its diff:
```python
import functools

import jax
import jax.numpy as jnp
from jax import lax
from jax.experimental import pallas as pl
from jax.experimental.pallas import tpu as pltpu
from jax.sharding import PartitionSpec as P

BF16 = jnp.bfloat16
F32 = jnp.float32
SLOTS = 8
LIMIT = 40 * 1024 * 1024

NN = (((1,), (0,)), ((), ()))
NT = (((1,), (1,)), ((), ()))
TN = (((0,), (0,)), ((), ()))


def mm(a, b, dims=NN):
    return lax.dot_general(a, b, dims, preferred_element_type=F32)


def vmem(count):
    return [pl.BlockSpec(memory_space=pltpu.VMEM)] * count


def call(kernel, outs, *args, scalars=0, scratch=()):
    specs = [pl.BlockSpec(memory_space=pltpu.SMEM)] * scalars + vmem(len(args) - scalars)
    return pl.pallas_call(
        kernel,
        out_shape=[jax.ShapeDtypeStruct(shape, dtype) for shape, dtype in outs],
        in_specs=specs,
        out_specs=vmem(len(outs)),
        scratch_shapes=list(scratch),
        compiler_params=pltpu.CompilerParams(vmem_limit_bytes=LIMIT),
    )(*args)


def pack_kernel(core_ref, gate_ref, up_ref, down_ref, own_ref, send_ref):
    width, hidden = gate_ref.shape
    half = hidden // 2
    quarter = half // 2
    for ref, which in ((own_ref, core_ref[0]), (send_ref, 1 - core_ref[0])):
        start = pl.multiple_of(which * half, half)
        ref[0:width, :] = gate_ref[:, pl.ds(start, half)]
        ref[width : 2 * width, :] = up_ref[:, pl.ds(start, half)]
        ref[2 * width :, :] = jnp.zeros((quarter, half), BF16)
        ref[2 * width :, 0:width] = down_ref[pl.ds(start, quarter), :]
        ref[2 * width :, quarter : quarter + width] = down_ref[
            pl.ds(pl.multiple_of(start + quarter, quarter), quarter), :
        ]


def route_kernel(ids_ref, weight_ref, token_ref, grad_ref, send_ref, mark_ref, scale_ref):
    tokens, picks = ids_ref.shape
    width = token_ref.shape[1]
    rows = mark_ref.shape[0]
    experts = rows // SLOTS
    side = send_ref.shape[1] // 2
    row_i = lax.broadcasted_iota(jnp.int32, (tokens, tokens), 0)
    col_i = lax.broadcasted_iota(jnp.int32, (tokens, tokens), 1)
    eye = (row_i == col_i).astype(F32)
    earlier = (row_i < col_i).astype(F32)
    ids = mm(ids_ref[...].astype(F32), eye, TN)
    weights = mm(weight_ref[...].astype(F32), eye, TN)
    expert_i = lax.broadcasted_iota(jnp.int32, (experts, tokens), 0).astype(F32)
    row_all = lax.broadcasted_iota(jnp.int32, (rows, tokens), 0).astype(F32)
    before = jnp.zeros((experts, 1), F32)
    marks, scales = [], []
    for pick in range(picks):
        hit = (expert_i == ids[pick : pick + 1, :]).astype(F32)
        count = mm(hit, earlier) + before
        slot = jnp.sum(hit * count, axis=0, keepdims=True)
        before = before + jnp.sum(hit, axis=1, keepdims=True)
        found = row_all == ids[pick : pick + 1, :] * SLOTS + slot
        marks.append(jnp.where(found, 1.0, 0.0))
        scales.append(jnp.where(found, weights[pick : pick + 1, :], 0.0))
    mark = jnp.concatenate([marks[0] + marks[1], marks[2] + marks[3]], axis=1).astype(BF16)
    scale = jnp.concatenate([scales[0] + scales[1], scales[2] + scales[3]], axis=1).astype(BF16)
    mark_ref[...] = mark
    scale_ref[...] = scale
    twice = lambda ref: jnp.concatenate([ref[...], ref[...]], axis=0)
    send_ref[...] = jnp.zeros_like(send_ref)
    send_ref[:, 0:width] = mm(mark, twice(token_ref)).astype(BF16)
    send_ref[:, side : side + width] = mm(scale, twice(grad_ref)).astype(BF16)


def slot_matrix(rows, kept, turned):
    sources = rows // SLOTS
    shape = (rows, kept) if turned else (kept, rows)
    small = lax.broadcasted_iota(jnp.int32, shape, 1 if turned else 0)
    large = lax.broadcasted_iota(jnp.int32, shape, 0 if turned else 1)
    return (lax.rem(small, sources) * SLOTS + small // sources == large).astype(BF16)


def sums_kernel(core_ref, rows_ref, own_ref, other_ref, sum_ref, kept_ref):
    rows, wide = rows_ref.shape[1:]
    kept = sum_ref.shape[0]
    side = wide // 2
    half = own_ref.shape[1]
    quarter = half // 2
    width = (own_ref.shape[0] - quarter) // 2
    pack = slot_matrix(rows, kept, False)
    mine = mm(pack, rows_ref[core_ref[0]]).astype(BF16)
    kept_ref[...] = mine
    theirs = mm(pack, rows_ref[1 - core_ref[0]]).astype(BF16)
    x_own, y_own = mine[:, 0:width], mine[:, side : side + width]
    x_other, y_other = theirs[:, 0:width], theirs[:, side : side + width]
    for part in range(2):
        lo = part * width
        sum_ref[:, part * half : (part + 1) * half] = mm(
            x_own, own_ref[lo : lo + width, :]
        ) + mm(x_other, other_ref[lo : lo + width, :])
    for part in range(2):
        lo = part * quarter
        sum_ref[:, 2 * half + lo : 2 * half + lo + quarter] = mm(
            y_own, own_ref[2 * width :, lo : lo + width], NT
        ) + mm(y_other, other_ref[2 * width :, lo : lo + width], NT)


def hidden_kernel(sum_ref, out_ref):
    half = sum_ref.shape[1] // 3
    gate = sum_ref[:, 0:half]
    up = sum_ref[:, half : 2 * half]
    back = sum_ref[:, 2 * half :]
    sig = jax.nn.sigmoid(gate)
    out_ref[:, 0:half] = (gate * sig * up).astype(BF16)
    out_ref[:, half : 2 * half] = (back * up * (sig * (1.0 + gate * (1.0 - sig)))).astype(BF16)
    out_ref[:, 2 * half :] = (back * (gate * sig)).astype(BF16)


def products_kernel(
    all_ref, kept_ref, gate_ref, up_ref, down_ref,
    send_ref, gate_sum_ref, up_sum_ref, down_sum_ref, hid_ref, dgate_ref, dup_ref, out_ref,
):
    kept, wide = kept_ref.shape
    side = wide // 2
    width, hidden = gate_ref.shape
    half = hidden // 2
    block = all_ref.shape[0] // 16
    for index in range(16):
        chip, core = index // 2, index % 2
        for part, ref in enumerate((hid_ref, dgate_ref, dup_ref)):
            ref[chip * block : (chip + 1) * block, core * half : (core + 1) * half] = all_ref[
                index * block : (index + 1) * block, part * half : (part + 1) * half
            ]
    out_ref[...] = jnp.zeros_like(out_ref)
    out_ref[:, 0:width] = mm(hid_ref[...], down_ref[...]).astype(BF16)
    out_ref[:, side : side + width] = (
        mm(dgate_ref[...], gate_ref[...], NT) + mm(dup_ref[...], up_ref[...], NT)
    ).astype(BF16)
    send_ref[...] = mm(slot_matrix(send_ref.shape[0], kept, True), out_ref[...]).astype(BF16)
    token_rows = kept_ref[:, 0:width]
    grad_rows = kept_ref[:, side : side + width]
    gate_sum_ref[...] = mm(token_rows, dgate_ref[...], TN).astype(BF16)
    up_sum_ref[...] = mm(token_rows, dup_ref[...], TN).astype(BF16)
    down_sum_ref[...] = mm(hid_ref[...], grad_rows, TN).astype(BF16)


def combine_kernel(back_ref, mark_ref, scale_ref, mixed_ref, token_grad_ref):
    tokens, width = mixed_ref.shape
    side = back_ref.shape[1] // 2
    for ref, marks, lo in ((mixed_ref, scale_ref, 0), (token_grad_ref, mark_ref, side)):
        parts = mm(marks[...], back_ref[:, lo : lo + width], TN).astype(BF16).astype(F32)
        ref[...] = (parts[0:tokens] + parts[tokens:]).astype(BF16)


def shards(tokens, expert_ids, route_weights, w_gate, w_up, w_down, grad_out):
    count, width = tokens.shape
    rep = lax.axis_size("rep")
    experts = lax.axis_size("node") * lax.axis_size("local")
    hidden = w_gate.shape[2]
    half, quarter = hidden // 2, hidden // 4
    side = -(-width // 128) * 128
    node_hits = 2 * count // lax.axis_size("node")
    mean_count = 2 * node_hits // lax.axis_size("local")
    depth = min(mean_count + max(mean_count // 2, 1), node_hits)
    kept = experts * depth
    rows = experts * SLOTS
    pairs = [[2 * i, 2 * i + 1] for i in range(rep // 2)]
    lines = [list(range(c, rep, 2)) for c in range(2)]
    core = (lax.axis_index("rep") % 2).astype(jnp.int32).reshape(1)
    gate_mat, up_mat, down_mat = w_gate[0], w_up[0], w_down[0]

    packed = ((2 * width + quarter, half), BF16)
    own, give = call(
        pack_kernel, [packed, packed], core, gate_mat, up_mat, down_mat, scalars=1
    )
    other = lax.ppermute(give, "rep", [(i, i ^ 1) for i in range(rep)])
    expert_ids, own = lax.optimization_barrier((expert_ids, own))
    send, mark, scale = call(
        route_kernel,
        [((rows, 2 * side), BF16), ((rows, 2 * count), BF16), ((rows, 2 * count), BF16)],
        expert_ids, route_weights, tokens, grad_out,
    )
    arrived = lax.all_to_all(
        send.reshape(experts, SLOTS, 2 * side), ("node", "local"), 0, 0, tiled=True
    )
    both = lax.all_gather(
        arrived.reshape(rows, 2 * side), "rep", axis=0, tiled=True, axis_index_groups=pairs
    )
    sums, kept_rows = call(
        sums_kernel,
        [((kept, 3 * half), F32), ((kept, 2 * side), BF16)],
        core, both.reshape(2, rows, 2 * side), own, other, scalars=1,
    )
    sums = lax.psum_scatter(
        sums, "rep", scatter_dimension=0, tiled=True, axis_index_groups=lines
    )
    (piece,) = call(hidden_kernel, [(sums.shape, BF16)], sums)
    whole = lax.all_gather(piece, "rep", axis=0, tiled=True)
    matrix = ((kept, hidden), BF16)
    send_back, gate_sum, up_sum, down_sum = call(
        products_kernel,
        [
            ((rows, 2 * side), BF16),
            (gate_mat.shape, BF16),
            (up_mat.shape, BF16),
            (down_mat.shape, BF16),
        ],
        whole, kept_rows, gate_mat, up_mat, down_mat,
        scratch=[pltpu.VMEM(*matrix)] * 3 + [pltpu.VMEM((kept, 2 * side), BF16)],
    )
    back = lax.all_to_all(
        send_back.reshape(experts, SLOTS, 2 * side), ("node", "local"), 0, 0, tiled=True
    )
    mixed, token_grad = call(
        combine_kernel,
        [(tokens.shape, BF16), (tokens.shape, BF16)],
        back.reshape(rows, 2 * side), mark, scale,
    )
    return (mixed, token_grad, gate_sum[None], up_sum[None], down_sum[None])


def solution(mesh):
    return jax.shard_map(
        shards,
        mesh=mesh,
        in_specs=(
            P(("node", "local"), "rep"),
            P(("node", "local"), None),
            P(("node", "local"), None),
            P(("node", "local"), "rep", None),
            P(("node", "local"), "rep", None),
            P(("node", "local"), None, "rep"),
            P(("node", "local"), "rep"),
        ),
        out_specs=(
            P(("node", "local"), "rep"),
            P(("node", "local"), "rep"),
            P(("node", "local"), "rep", None),
            P(("node", "local"), "rep", None),
            P(("node", "local"), None, "rep"),
        ),
        check_vma=False,
    )
```

time: 344 us -> 218 us (0.63)
  the two profiles are of different devices: /device:TPU:16 before, /device:TPU:4 now
where the time goes in v1:
time: 218 us; the launch traced here: 217 us
  waiting for transfers between devices  139 us (64%)
  blocking collectives  32.9 us (15%)
  starting transfers between devices  14.8 us (7%)
  between operations  13.8 us (6%)
  local copies, waits for them, and re-layouts  8.97 us (4%)
  Pallas kernels  7.81 us (4%)
    reduce_scatter x1, waiting for transfers between devices, shards(): lax.psum_scatter(sums, 'rep', scatter_dimension=0, tiled=True, axis_index...  52.7 us
    all_gather x1, waiting for transfers between devices, shards(): whole = lax.all_gather(piece, 'rep', axis=0, tiled=True)  46.1 us
    all_to_all x1, blocking collectives, shards(): lax.all_to_all(send.reshape(experts, SLOTS, 2 * side), ('node', 'local'),...  32.9 us
    all_to_all x1, waiting for transfers between devices, shards(): lax.all_to_all(send_back.reshape(experts, SLOTS, 2 * side), ('node', 'loc...  18.9 us
    all_gather x1, waiting for transfers between devices, shards(): lax.all_gather(arrived.reshape(rows, 2 * side), 'rep', axis=0, tiled=True...  18.7 us
    all_to_all x1, starting transfers between devices, shards(): lax.all_to_all(send_back.reshape(experts, SLOTS, 2 * side), ('node', 'loc...  12.8 us
    unnamed x23, local copies, waits for them, and re-layouts  8.88 us
    pallas_call x6, Pallas kernels, call(): pl.pallas_call(kernel, out_shape=[jax.ShapeDtypeStruct(shape, dtype) for...  7.81 us
  transfers between devices with their start and end apart: 5, of which 5 were waited for; matrix products, arithmetic and copies ran while one was open for 0% of the time, Pallas kernels for 0%

profile of v1, /device:TPU:4, one launch (start us, length us, event | category | flops | bytes accessed | tf_op | source)
XLA Modules:
  0.0 217.0 jit_solution(11523790553418714215)
XLA Ops:
  7.2 0.0 copy-start.9
  7.2 0.0 copy-start.8
  7.2 0.0 copy-start.7
  7.2 0.0 all-gather.3.cloned.1.call-start
  7.2 0.8 copy.14.weight_ref
  8.0 1.2 copy.12
  9.3 0.0 copy-start.1
  9.3 1.0 copy-done.1
  10.3 0.0 copy-start.3
  10.3 1.0 copy-done.3
  11.3 0.1 shard_map.110
  11.4 0.0 copy-done.9
  11.5 0.1 copy.13.ids_ref
  11.5 0.0 copy-done.8
  11.6 0.0 copy-done.7
  11.6 0.7 shard_map.111
  12.3 32.9 %all_to_all.10 = bf16[64,8,512]{2,1,0:T(8,128)(2,1)} all-to-all(bf16[64,8,512]{2,1,0:T(8,128)(2,1)S(1)} %bitcast.20), channel_id=1, replica_groups=mesh['rep'=16,'node'=8,'local'=8] {'node','local'}, dimensions={0} | all-to-all | bytes 1048576 | tf_op jit(solution)/shard_map/all_to_all | solution.py:197
  45.2 0.0 all-gather.3.cloned.1.call-update
  45.2 0.0 reduce-scatter.2.cloned.1.call-start
  45.2 1.9 collective-permute-start
  47.2 2.2 collective-permute-done.other_ref
  49.3 18.7 %all-gather.3.cloned.1.call-done = bf16[1024,512]{1,0:T(8,128)(2,1)} async-done(((bf16[512,512]{1,0:T(8,128)(2,1)}), bf16[1024,512]{1,0:T(8,128)(2,1)}) %all-gather.3.cloned.1.call-update) | async-done | bytes 1048592 | tf_op jit(solution)/shard_map/all_gather | solution.py:200
  68.0 0.0 copy-start.5
  68.0 1.2 copy-done.5
  69.2 0.0 copy-start.2
  69.2 0.0 copy-start.4
  69.2 2.7 %shard_map.112 = (f32[384,1536]{1,0:T(8,128)}, bf16[384,512]{1,0:T(8,128)(2,1)S(1)}) custom-call(s32[1]{0:T(128)} %bitcast.core_ref, bf16[2,512,512]{2,1,0:T(8,128)(2,1)S(1)} %bitcast.19, bf16[704,512]{1,0:T(8,128)(2,1)S(1)} %get-tuple-element.23.own_ref, bf16[704,512]{1,0:T(8,128)(2,1)S(1)} %collective-permute-done.other_ref), custom_call_target="tpu_custom_call" | custom-call | tf_op jit(solution)/shard_map/pallas_call | solution.py:30
  71.9 0.0 reduce-scatter.2.cloned.1.call-update
  71.9 0.0 all-gather.5.cloned.1.call-start
  72.0 52.7 %reduce-scatter.2.cloned.1.call-done.sum_ref = f32[48,1536]{1,0:T(8,128)} async-done(((f32[384,1536]{1,0:T(8,128)}), f32[48,1536]{1,0:T(8,128)}) %reduce-scatter.2.cloned.1.call-update) | async-done | bytes 294928 | tf_op jit(solution)/shard_map/reduce_scatter | solution.py:208
  124.7 0.0 copy-start.6
  124.7 1.0 copy-done.6
  125.7 0.7 shard_map.113
  126.4 0.0 all-gather.5.cloned.1.call-update
  126.4 46.1 %all-gather.5.cloned.1.call-done.all_ref = bf16[768,1536]{1,0:T(8,128)(2,1)} async-done(((bf16[48,1536]{1,0:T(8,128)(2,1)}), bf16[768,1536]{1,0:T(8,128)(2,1)}) %all-gather.5.cloned.1.call-update) | async-done | bytes 2359312 | tf_op jit(solution)/shard_map/all_gather | solution.py:212
  172.6 0.0 copy-done.2
  172.6 0.0 copy-done.4
  172.6 0.0 copy-start
  172.6 1.7 copy-done
  174.2 2.7 %shard_map.114 = (bf16[512,512]{1,0:T(8,128)(2,1)}, bf16[224,1024]{1,0:T(8,128)(2,1)}, bf16[224,1024]{1,0:T(8,128)(2,1)}, bf16[1024,224]{1,0:T(8,128)(2,1)S(1)}) custom-call(bf16[768,1536]{1,0:T(8,128)(2,1)S(1)} %copy-done, bf16[384,512]{1,0:T(8,128)(2,1)S(1)} %get-tuple-element.26.kept_ref, bf16[224,1024]{1,0:T(8,128)(2,1)S(1)} %bitcast.16, ...), custom_call_target="tpu_custom_call" | custom-call | tf_op jit(solution)/shard_map/pallas_call | solution.py:30
  176.9 12.8 %all-to-all-start.1 = ((bf16[64,8,512]{2,1,0:T(8,128)(2,1)}), bf16[64,8,512]{2,1,0:T(8,128)(2,1)S(1)}, u32[]{:S(2)}, u32[]{:S(2)}) async-start(bf16[64,8,512]{2,1,0:T(8,128)(2,1)} %bitcast.7), calls=%async_computation.2 | async-start | bytes 1048576 | tf_op jit(solution)/shard_map/all_to_all | solution.py:225
  189.7 1.0 copy.15
  190.7 18.9 %all-to-all-done.1 = bf16[64,8,512]{2,1,0:T(8,128)(2,1)S(1)} async-done(((bf16[64,8,512]{2,1,0:T(8,128)(2,1)}), bf16[64,8,512]{2,1,0:T(8,128)(2,1)S(1)}, u32[]{:S(2)}, u32[]{:S(2)}) %all-to-all-start.1) | async-done | bytes 524320 | tf_op jit(solution)/shard_map/all_to_all | solution.py:225
  209.5 0.9 shard_map.115
Async XLA Ops:
  7.2 4.3 %copy-start.9 = (s32[64,4]{0,1:T(4,128)S(1)}, s32[64,4]{0,1:T(4,128)}, u32[]{:S(2)}) copy-start(s32[64,4]{0,1:T(4,128)} %param.8) | copy-start | bytes 3076
  7.2 4.4 %copy-start.8 = (bf16[64,224]{1,0:T(8,128)(2,1)S(1)}, bf16[64,224]{1,0:T(8,128)(2,1)}, u32[]{:S(2)}) copy-start(bf16[64,224]{1,0:T(8,128)(2,1)} %grad_ref.1) | copy-start | bytes 86020
  7.2 4.4 %copy-start.7 = (bf16[64,224]{1,0:T(8,128)(2,1)S(1)}, bf16[64,224]{1,0:T(8,128)(2,1)}, u32[]{:S(2)}) copy-start(bf16[64,224]{1,0:T(8,128)(2,1)} %token_ref.1) | copy-start | bytes 86020
  7.2 60.8 %all-gather.3.cloned.1.call-start = ((), (), s32[]{:S(2)}) async-start(), calls=%async_computation.3 | async-start | bytes 1572864 | tf_op jit(solution)/shard_map/all_gather | solution.py:200
  9.3 1.0 copy-start.1
  10.3 1.0 copy-start.3
  45.2 79.5 %reduce-scatter.2.cloned.1.call-start = ((), (), s32[]{:S(2)}) async-start(), calls=%async_computation.4 | async-start | bytes 2654208 | tf_op jit(solution)/shard_map/reduce_scatter | solution.py:208
  45.2 4.1 %collective-permute-start = (bf16[704,512]{1,0:T(8,128)(2,1)S(1)}, bf16[704,512]{1,0:T(8,128)(2,1)S(1)}, u32[]{:S(2)}, u32[]{:S(2)}) collective-permute-start(bf16[704,512]{1,0:T(8,128)(2,1)S(1)} %get-tuple-element.24), channel_id=1, source_target_pairs={{0,64},{64,0},{128,192},{192,128},{256,320},{320,256},{384,448},{4... | collective-permute-start | bytes 2162696 | tf_op jit(solution)/shard_map/ppermute | solution.py:190
  68.0 1.2 copy-start.5
  69.2 103.3 %copy-start.2 = (bf16[1,224,1024]{2,1,0:T(8,128)(2,1)S(1)}, bf16[1,224,1024]{2,1,0:T(8,128)(2,1)}, u32[]{:S(2)}) copy-start(bf16[1,224,1024]{2,1,0:T(8,128)(2,1)} %param.10) | copy-start | bytes 1376260
  69.2 103.3 %copy-start.4 = (bf16[1,224,1024]{2,1,0:T(8,128)(2,1)S(1)}, bf16[1,224,1024]{2,1,0:T(8,128)(2,1)}, u32[]{:S(2)}) copy-start(bf16[1,224,1024]{2,1,0:T(8,128)(2,1)} %param.11) | copy-start | bytes 1376260
  71.9 100.6 %all-gather.5.cloned.1.call-start = ((), (), s32[]{:S(2)}) async-start(), calls=%async_computation.5 | async-start | bytes 2506752 | tf_op jit(solution)/shard_map/all_gather | solution.py:212
  124.7 1.0 copy-start.6
  172.6 1.7 copy-start
  176.9 32.6 %all-to-all-start.1 = ((bf16[64,8,512]{2,1,0:T(8,128)(2,1)}), bf16[64,8,512]{2,1,0:T(8,128)(2,1)S(1)}, u32[]{:S(2)}, u32[]{:S(2)}) async-start(bf16[64,8,512]{2,1,0:T(8,128)(2,1)} %bitcast.7), calls=%async_computation.2 | async-start | bytes 1048576 | tf_op jit(solution)/shard_map/all_to_all | solution.py:225
Sparse Core Ops, SparseCore 0:
  45.3 22.6 all-gather.2
  72.1 52.6 reduce-scatter.1
  128.0 44.5 all-gather.4

commit v2 on v1

v2 whole, which is shorter than its diff:
```python
import jax
import jax.numpy as jnp
from jax import lax
from jax.experimental import pallas as pl
from jax.experimental.pallas import tpu as pltpu
from jax.sharding import PartitionSpec as P

BF16 = jnp.bfloat16
F32 = jnp.float32
SLOTS = 8
LIMIT = 40 * 1024 * 1024

NN = (((1,), (0,)), ((), ()))
NT = (((1,), (1,)), ((), ()))
TN = (((0,), (0,)), ((), ()))


def mm(a, b, dims=NN):
    return lax.dot_general(a, b, dims, preferred_element_type=F32)


def vmem(count):
    return [pl.BlockSpec(memory_space=pltpu.VMEM)] * count


def call(kernel, outs, *args, scalars=0, scratch=()):
    specs = [pl.BlockSpec(memory_space=pltpu.SMEM)] * scalars + vmem(len(args) - scalars)
    return pl.pallas_call(
        kernel,
        out_shape=[jax.ShapeDtypeStruct(shape, dtype) for shape, dtype in outs],
        in_specs=specs,
        out_specs=vmem(len(outs)),
        scratch_shapes=list(scratch),
        compiler_params=pltpu.CompilerParams(vmem_limit_bytes=LIMIT),
    )(*args)


def pack_kernel(core_ref, gate_ref, up_ref, down_ref, own_ref, send_ref):
    width, hidden = gate_ref.shape
    half = hidden // 2
    for ref, which in ((own_ref, core_ref[0]), (send_ref, 1 - core_ref[0])):
        start = pl.multiple_of(which * half, half)
        for part, mat_ref in enumerate((gate_ref, up_ref, down_ref)):
            ref[part * width : (part + 1) * width, :] = mat_ref[:, pl.ds(start, half)]


def route_kernel(ids_ref, weight_ref, token_ref, grad_ref, send_ref, mark_ref, scale_ref):
    picks, tokens = ids_ref.shape
    width = token_ref.shape[1]
    rows = mark_ref.shape[0]
    experts = rows // SLOTS
    side = send_ref.shape[1] // 2
    row_i = lax.broadcasted_iota(jnp.int32, (tokens, tokens), 0)
    col_i = lax.broadcasted_iota(jnp.int32, (tokens, tokens), 1)
    earlier = (row_i < col_i).astype(F32)
    ids = ids_ref[...].astype(F32)
    weights = weight_ref[...].astype(F32)
    expert_i = lax.broadcasted_iota(jnp.int32, (experts, tokens), 0).astype(F32)
    row_all = lax.broadcasted_iota(jnp.int32, (rows, tokens), 0).astype(F32)
    before = jnp.zeros((experts, 1), F32)
    marks, scales = [], []
    for pick in range(picks):
        hit = (expert_i == ids[pick : pick + 1, :]).astype(F32)
        count = mm(hit, earlier) + before
        slot = jnp.sum(hit * count, axis=0, keepdims=True)
        before = before + jnp.sum(hit, axis=1, keepdims=True)
        found = row_all == ids[pick : pick + 1, :] * SLOTS + slot
        marks.append(jnp.where(found, 1.0, 0.0))
        scales.append(jnp.where(found, weights[pick : pick + 1, :], 0.0))
    mark = jnp.concatenate([marks[0] + marks[1], marks[2] + marks[3]], axis=1).astype(BF16)
    scale = jnp.concatenate([scales[0] + scales[1], scales[2] + scales[3]], axis=1).astype(BF16)
    mark_ref[...] = mark
    scale_ref[...] = scale
    twice = lambda ref: jnp.concatenate([ref[...], ref[...]], axis=0)
    send_ref[...] = jnp.zeros_like(send_ref)
    send_ref[:, 0:width] = mm(mark, twice(token_ref)).astype(BF16)
    send_ref[:, side : side + width] = mm(scale, twice(grad_ref)).astype(BF16)


def slot_matrix(rows, kept, turned):
    sources = rows // SLOTS
    shape = (rows, kept) if turned else (kept, rows)
    small = lax.broadcasted_iota(jnp.int32, shape, 1 if turned else 0)
    large = lax.broadcasted_iota(jnp.int32, shape, 0 if turned else 1)
    return (lax.rem(small, sources) * SLOTS + small // sources == large).astype(BF16)


def sums_kernel(mine_ref, theirs_ref, own_ref, other_ref, sum_ref, kept_ref):
    rows, wide = mine_ref.shape
    kept = sum_ref.shape[0]
    side = wide // 2
    half = own_ref.shape[1]
    width = own_ref.shape[0] // 3
    pack = slot_matrix(rows, kept, False)
    mine = mm(pack, mine_ref[...]).astype(BF16)
    kept_ref[...] = mine
    theirs = mm(pack, theirs_ref[...]).astype(BF16)
    for part, lo in enumerate((0, 0, side)):
        block = slice(part * width, (part + 1) * width)
        sum_ref[:, part * half : (part + 1) * half] = (
            mm(mine[:, lo : lo + width], own_ref[block, :])
            + mm(theirs[:, lo : lo + width], other_ref[block, :])
        ).astype(BF16)


def hidden_kernel(sum_ref, hid_ref, dgate_ref, dup_ref):
    half = sum_ref.shape[2] // 3
    total = lambda part: jnp.sum(
        sum_ref[:, :, part * half : (part + 1) * half].astype(F32), axis=0
    )
    gate, up, back = total(0), total(1), total(2)
    sig = jax.nn.sigmoid(gate)
    hid = (gate * sig * up).astype(BF16)
    for peer in range(hid_ref.shape[0]):
        hid_ref[peer] = hid
    dgate_ref[...] = (back * up * (sig * (1.0 + gate * (1.0 - sig)))).astype(BF16)
    dup_ref[...] = (back * (gate * sig)).astype(BF16)


def rows_kernel(
    core_ref, own_ref, other_ref, dgates_ref, dups_ref, gate_ref, up_ref, down_ref,
    send_ref, hid_ref, dgate_ref, dup_ref, out_ref,
):
    kept, hidden = hid_ref.shape
    half = hidden // 2
    width = gate_ref.shape[0]
    side = out_ref.shape[1] // 2
    block = dgates_ref.shape[0] // 16
    for ref, which in ((own_ref, core_ref[0]), (other_ref, 1 - core_ref[0])):
        hid_ref[:, pl.ds(pl.multiple_of(which * half, half), half)] = ref[...]
    for index in range(16):
        chip, core = index // 2, index % 2
        for ref, piece_ref in ((dgate_ref, dgates_ref), (dup_ref, dups_ref)):
            ref[chip * block : (chip + 1) * block, core * half : (core + 1) * half] = piece_ref[
                index * block : (index + 1) * block, :
            ]
    out_ref[...] = jnp.zeros_like(out_ref)
    out_ref[:, 0:width] = mm(hid_ref[...], down_ref[...], NT).astype(BF16)
    out_ref[:, side : side + width] = (
        mm(dgate_ref[...], gate_ref[...], NT) + mm(dup_ref[...], up_ref[...], NT)
    ).astype(BF16)
    send_ref[...] = mm(slot_matrix(send_ref.shape[0], kept, True), out_ref[...]).astype(BF16)


def weights_kernel(
    kept_ref, hid_ref, dgate_ref, dup_ref, gate_sum_ref, up_sum_ref, down_sum_ref
):
    width = gate_sum_ref.shape[0]
    side = kept_ref.shape[1] // 2
    token_rows = kept_ref[:, 0:width]
    grad_rows = kept_ref[:, side : side + width]
    gate_sum_ref[...] = mm(token_rows, dgate_ref[...], TN).astype(BF16)
    up_sum_ref[...] = mm(token_rows, dup_ref[...], TN).astype(BF16)
    down_sum_ref[...] = mm(grad_rows, hid_ref[...], TN).astype(BF16)


def combine_kernel(back_ref, mark_ref, scale_ref, mixed_ref, token_grad_ref):
    tokens, width = mixed_ref.shape
    side = back_ref.shape[1] // 2
    for ref, marks, lo in ((mixed_ref, scale_ref, 0), (token_grad_ref, mark_ref, side)):
        parts = mm(marks[...], back_ref[:, lo : lo + width], TN).astype(BF16).astype(F32)
        ref[...] = (parts[0:tokens] + parts[tokens:]).astype(BF16)


def shards(tokens, expert_ids, route_weights, w_gate, w_up, w_down, grad_out):
    count, width = tokens.shape
    rep = lax.axis_size("rep")
    experts = lax.axis_size("node") * lax.axis_size("local")
    hidden = w_gate.shape[2]
    half = hidden // 2
    side = -(-width // 128) * 128
    node_hits = 2 * count // lax.axis_size("node")
    mean_count = 2 * node_hits // lax.axis_size("local")
    depth = min(mean_count + max(mean_count // 2, 1), node_hits)
    kept = experts * depth
    rows = experts * SLOTS
    lines = [list(range(c, rep, 2)) for c in range(2)]
    chips = rep // 2
    swap = [(i, i ^ 1) for i in range(rep)]
    core = (lax.axis_index("rep") % 2).astype(jnp.int32).reshape(1)
    gate_mat, up_mat, down_mat = w_gate[0], w_up[0], w_down[0].T

    send, mark, scale = call(
        route_kernel,
        [((rows, 2 * side), BF16), ((rows, 2 * count), BF16), ((rows, 2 * count), BF16)],
        expert_ids.T, route_weights.T, tokens, grad_out,
    )
    mine = lax.all_to_all(
        send.reshape(experts, SLOTS, 2 * side), ("node", "local"), 0, 0, tiled=True
    ).reshape(rows, 2 * side)
    packed = ((3 * width, half), BF16)
    own, give = call(
        pack_kernel, [packed, packed], core, gate_mat, up_mat, down_mat, scalars=1
    )
    other = lax.ppermute(give, "rep", swap)
    theirs = lax.ppermute(mine, "rep", swap)
    sums, kept_rows = call(
        sums_kernel,
        [((kept, 3 * half), BF16), ((kept, 2 * side), BF16)],
        mine, theirs, own, other,
    )
    sums = lax.all_to_all(
        sums.reshape(chips, kept // chips, 3 * half),
        "rep", 0, 0, tiled=True, axis_index_groups=lines,
    )
    piece = ((kept // chips, half), BF16)
    hid, dgate, dup = call(
        hidden_kernel, [((chips,) + piece[0], BF16), piece, piece], sums
    )
    hid_own = lax.all_to_all(
        hid, "rep", 0, 0, tiled=True, axis_index_groups=lines
    ).reshape(kept, half)
    dgates = lax.all_gather(dgate, "rep", axis=0, tiled=True)
    dgates, dup, hid_own = lax.optimization_barrier((dgates, dup, hid_own))
    hid_other = lax.ppermute(hid_own, "rep", swap)
    dups = lax.all_gather(dup, "rep", axis=0, tiled=True)
    matrix = ((kept, hidden), BF16)
    send_back, hid, dgate, dup = call(
        rows_kernel,
        [((rows, 2 * side), BF16), matrix, matrix, matrix],
        core, hid_own, hid_other, dgates, dups, gate_mat, up_mat, down_mat,
        scalars=1,
        scratch=[pltpu.VMEM((kept, 2 * side), BF16)],
    )
    back = lax.all_to_all(
        send_back.reshape(experts, SLOTS, 2 * side), ("node", "local"), 0, 0, tiled=True
    )
    grads = ((width, hidden), BF16)
    gate_sum, up_sum, down_sum = call(
        weights_kernel, [grads, grads, grads], kept_rows, hid, dgate, dup
    )
    mixed, token_grad = call(
        combine_kernel,
        [(tokens.shape, BF16), (tokens.shape, BF16)],
        back.reshape(rows, 2 * side), mark, scale,
    )
    return (mixed, token_grad, gate_sum[None], up_sum[None], down_sum.T[None])


def solution(mesh):
    return jax.shard_map(
        shards,
        mesh=mesh,
        in_specs=(
            P(("node", "local"), "rep"),
            P(("node", "local"), None),
            P(("node", "local"), None),
            P(("node", "local"), "rep", None),
            P(("node", "local"), "rep", None),
            P(("node", "local"), None, "rep"),
            P(("node", "local"), "rep"),
        ),
        out_specs=(
            P(("node", "local"), "rep"),
            P(("node", "local"), "rep"),
            P(("node", "local"), "rep", None),
            P(("node", "local"), "rep", None),
            P(("node", "local"), None, "rep"),
        ),
        check_vma=False,
    )
```

time: 218 us -> 171 us (0.78)
  waiting for transfers between devices: 139 us -> 29.8 us
  blocking collectives: 32.9 us -> 88.7 us
  starting transfers between devices: 14.8 us -> 32.3 us
  between operations: 13.8 us -> 0.81 us
    all_gather x2 -> x0, waiting for transfers between devices: 64.8 us -> none  [the longest x1 46.1 us: shards(): whole = lax.all_gather(piece, 'rep', axis=0, tiled=True)]
    reduce_scatter x1 -> x0, waiting for transfers between devices: 52.7 us -> none  [shards(): lax.psum_scatter(sums, 'rep', scatter_dimension=0, tiled=True, axis_index...]
    all_gather x0 -> x2, blocking collectives: none -> 40.4 us  [the longest x1 23.6 us: shards(): dgates = lax.all_gather(dgate, 'rep', axis=0, tiled=True)]
    all_to_all x0 -> x2, starting transfers between devices: none -> 20.9 us  [the longest x1 17.3 us: shards(): lax.all_to_all(send.reshape(experts, SLOTS, 2 * side), ('node', 'local'),...]
    all_to_all x1, blocking collectives: 32.9 us -> 48.2 us  [shards(): lax.all_to_all(sums.reshape(chips, kept // chips, 3 * half), 'rep', 0, 0,...]
    all_to_all x0 -> x2, waiting for transfers between devices: none -> 11.8 us  [the longest x1 11.8 us: shards(): lax.all_to_all(send.reshape(experts, SLOTS, 2 * side), ('node', 'local'),...]
    all_to_all x1, starting transfers between devices: 12.8 us -> 5.35 us  [shards(): lax.all_to_all(send_back.reshape(experts, SLOTS, 2 * side), ('node', 'loc...]
    ppermute x1 -> x3, starting transfers between devices: 1.92 us -> 6.06 us  [the longest x1 2.25 us: shards(): hid_other = lax.ppermute(hid_own, 'rep', swap)]
  transfers between devices with their start and end apart: 5 -> 6, of which waited for: 5 -> 3; matrix products, arithmetic and copies ran while one was open for 0% -> 0% of each run, Pallas kernels for 0% -> 2%
where the time goes in v2:
time: 171 us; the launch traced here: 170 us
  blocking collectives  88.7 us (52%)
  starting transfers between devices  32.3 us (19%)
  waiting for transfers between devices  29.8 us (17%)
  local copies, waits for them, and re-layouts  10.1 us (6%)
  Pallas kernels  8.51 us (5%)
    all_to_all x1, blocking collectives, shards(): lax.all_to_all(sums.reshape(chips, kept // chips, 3 * half), 'rep', 0, 0,...  48.2 us
    all_gather x1, blocking collectives, shards(): dgates = lax.all_gather(dgate, 'rep', axis=0, tiled=True)  23.6 us
    all_to_all x1, starting transfers between devices, shards(): lax.all_to_all(send.reshape(experts, SLOTS, 2 * side), ('node', 'local'),...  17.3 us
    all_gather x1, blocking collectives, shards(): dups = lax.all_gather(dup, 'rep', axis=0, tiled=True)  16.9 us
    all_to_all x1, waiting for transfers between devices, shards(): lax.all_to_all(send_back.reshape(experts, SLOTS, 2 * side), ('node', 'loc...  16.1 us
    all_to_all x1, waiting for transfers between devices, shards(): lax.all_to_all(send.reshape(experts, SLOTS, 2 * side), ('node', 'local'),...  11.8 us
    unnamed x34, local copies, waits for them, and re-layouts  10.1 us
    pallas_call x7, Pallas kernels, call(): pl.pallas_call(kernel, out_shape=[jax.ShapeDtypeStruct(shape, dtype) for...  8.51 us
  transfers between devices with their start and end apart: 6, of which 3 were waited for; matrix products, arithmetic and copies ran while one was open for 0% of the time, Pallas kernels for 2%

profile of v2, /device:TPU:4, one launch (start us, length us, event | category | flops | bytes accessed | tf_op | source)
XLA Modules:
  0.0 170.2 jit_solution(11488538970919906130)
XLA Ops:
  0.6 0.0 copy-start.1
  0.6 0.0 copy-start
  0.7 0.0 copy-start.13
  0.7 0.8 copy-done.13
  1.5 0.0 copy-start.14
  1.5 0.8 copy-done.14
  2.2 0.0 copy-start.15
  2.3 0.7 copy-done.15
  2.9 0.7 copy-done.16
  3.6 1.4 shard_map.110
  5.0 0.6 copy-done.11
  5.7 17.3 %all-to-all-start = ((bf16[64,8,512]{2,1,0:T(8,128)(2,1)}), bf16[64,8,512]{2,1,0:T(8,128)(2,1)S(1)}, u32[]{:S(2)}, u32[]{:S(2)}) async-start(bf16[64,8,512]{2,1,0:T(8,128)(2,1)} %bitcast.3), calls=%async_computation | async-start | bytes 1048576 | tf_op jit(solution)/shard_map/all_to_all | solution.py:188
  23.0 0.0 copy-done.1
  23.0 0.0 copy-done
  23.0 0.0 copy-start.2
  23.0 1.0 copy-done.2
  24.0 0.9 shard_map.111
  25.0 1.9 %collective-permute-start.1 = (bf16[672,512]{1,0:T(8,128)(2,1)}, bf16[672,512]{1,0:T(8,128)(2,1)S(1)}, u32[]{:S(2)}, u32[]{:S(2)}) collective-permute-start(bf16[672,512]{1,0:T(8,128)(2,1)} %get-tuple-element.29), channel_id=1, source_target_pairs={{0,64},{64,0},{128,192},{192,128},{256,320},{320,256},{384,448},{4... | collective-permute-start | bytes 2064392 | tf_op jit(solution)/shard_map/ppermute | solution.py:195
  26.9 11.8 %all-to-all-done = bf16[64,8,512]{2,1,0:T(8,128)(2,1)S(1)} async-done(((bf16[64,8,512]{2,1,0:T(8,128)(2,1)}), bf16[64,8,512]{2,1,0:T(8,128)(2,1)S(1)}, u32[]{:S(2)}, u32[]{:S(2)}) %all-to-all-start) | async-done | bytes 524320 | tf_op jit(solution)/shard_map/all_to_all | solution.py:188
  38.7 1.9 %collective-permute-start = (bf16[512,512]{1,0:T(8,128)(2,1)S(1)}, bf16[512,512]{1,0:T(8,128)(2,1)S(1)}, u32[]{:S(2)}, u32[]{:S(2)}) collective-permute-start(bf16[512,512]{1,0:T(8,128)(2,1)S(1)} %bitcast.19), channel_id=1, source_target_pairs={{0,64},{64,0},{128,192},{192,128},{256,320},{320,256},{384,448},{4... | collective-permute-start | bytes 1572872 | tf_op jit(solution)/shard_map/ppermute | solution.py:196
  40.6 0.0 collective-permute-done.1.other_ref
  40.6 1.9 %collective-permute-done.theirs_ref = bf16[512,512]{1,0:T(8,128)(2,1)S(1)} collective-permute-done((bf16[512,512]{1,0:T(8,128)(2,1)S(1)}, bf16[512,512]{1,0:T(8,128)(2,1)S(1)}, u32[]{:S(2)}, u32[]{:S(2)}) %collective-permute-start) | collective-permute-done | bytes 524320 | tf_op jit(solution)/shard_map/ppermute | solution.py:196
  42.5 1.2 shard_map.112
  43.7 0.0 copy-start.9
  43.7 0.7 copy-done.9
  44.5 48.2 %all_to_all.20.sum_ref = bf16[8,48,1536]{2,1,0:T(8,128)(2,1)S(1)} all-to-all(bf16[8,48,1536]{2,1,0:T(8,128)(2,1)S(1)} %bitcast.30), channel_id=1, replica_groups={{0,128,256,384,512,640,768,896},{64,192,320,448,576,704,832,960},{1,129..., dimensions={0} | all-to-all | bytes 2359296 | tf_op jit(solution)/shard_map/all_to_all | solution.py:202
  92.7 0.9 shard_map.113
  93.6 3.6 %all-to-all-start.2 = ((bf16[8,48,512]{2,1,0:T(8,128)(2,1)}), bf16[8,48,512]{2,1,0:T(8,128)(2,1)S(1)}, u32[]{:S(2)}, u32[]{:S(2)}) async-start(bf16[8,48,512]{2,1,0:T(8,128)(2,1)} %get-tuple-element.33), calls=%async_computation.2 | async-start | bytes 786432 | tf_op jit(solution)/shard_map/all_to_all | solution.py:210
  97.2 23.6 %all_gather.6.dgates_ref = bf16[768,512]{1,0:T(8,128)(2,1)S(1)} all-gather(bf16[48,512]{1,0:T(8,128)(2,1)S(1)} %get-tuple-element.31), channel_id=1, replica_groups=mesh['rep'=16,'node'=8,'local'=8] {'rep'}, dimensions={0}, use_global_device_ids=true | all-gather | bytes 835584 | tf_op jit(solution)/shard_map/all_gather | solution.py:213
  120.7 0.0 all-to-all-done.2
  120.7 2.2 %collective-permute-start.2 = (bf16[384,512]{1,0:T(8,128)(2,1)S(1)}, bf16[384,512]{1,0:T(8,128)(2,1)S(1)}, u32[]{:S(2)}, u32[]{:S(2)}) collective-permute-start(bf16[384,512]{1,0:T(8,128)(2,1)S(1)} %bitcast.28), channel_id=1, source_target_pairs={{0,64},{64,0},{128,192},{192,128},{256,320},{320,256},{384,448},{4... | collective-permute-start | bytes 1179656 | tf_op jit(solution)/shard_map/ppermute | solution.py:215
  123.0 16.9 %all_gather.7.dups_ref = bf16[768,512]{1,0:T(8,128)(2,1)S(1)} all-gather(bf16[48,512]{1,0:T(8,128)(2,1)S(1)} %get-tuple-element.36), channel_id=1, replica_groups=mesh['rep'=16,'node'=8,'local'=8] {'rep'}, dimensions={0}, use_global_device_ids=true | all-gather | bytes 835584 | tf_op jit(solution)/shard_map/all_gather | solution.py:216
  139.8 0.0 collective-permute-done.2.other_ref
  139.8 0.0 copy-done.3
  139.8 1.5 shard_map.114
  141.4 0.0 copy-start.4
  141.4 0.9 copy-done.4
  142.3 0.9 copy-done.6
  143.2 0.8 copy-done.8
  144.0 5.3 %all-to-all-start.3 = ((bf16[64,8,512]{2,1,0:T(8,128)(2,1)}), bf16[64,8,512]{2,1,0:T(8,128)(2,1)S(1)}, u32[]{:S(2)}, u32[]{:S(2)}) async-start(bf16[64,8,512]{2,1,0:T(8,128)(2,1)} %bitcast.31), calls=%async_computation.3 | async-start | bytes 1048576 | tf_op jit(solution)/shard_map/all_to_all | solution.py:225
  149.3 0.0 copy-done.5
  149.4 0.0 copy-start.7
  149.4 1.1 copy-done.7
  150.5 1.0 copy-done.10
  151.5 1.7 shard_map.116
  153.2 16.1 %all-to-all-done.3 = bf16[64,8,512]{2,1,0:T(8,128)(2,1)S(1)} async-done(((bf16[64,8,512]{2,1,0:T(8,128)(2,1)}), bf16[64,8,512]{2,1,0:T(8,128)(2,1)S(1)}, u32[]{:S(2)}, u32[]{:S(2)}) %all-to-all-start.3) | async-done | bytes 524320 | tf_op jit(solution)/shard_map/all_to_all | solution.py:225
  169.3 0.0 copy-done.12
  169.3 0.9 shard_map.115
  (8 shorter events, 0.0 us)
Async XLA Ops:
  0.6 22.4 %copy-start.1 = (bf16[1,224,1024]{2,1,0:T(8,128)(2,1)S(1)}, bf16[1,224,1024]{2,1,0:T(8,128)(2,1)}, u32[]{:S(2)}) copy-start(bf16[1,224,1024]{2,1,0:T(8,128)(2,1)} %param.11) | copy-start | bytes 1376260
  0.6 22.4 %copy-start = (bf16[1,224,1024]{2,1,0:T(8,128)(2,1)S(1)}, bf16[1,224,1024]{2,1,0:T(8,128)(2,1)}, u32[]{:S(2)}) copy-start(bf16[1,224,1024]{2,1,0:T(8,128)(2,1)} %param.10) | copy-start | bytes 1376260
  0.7 0.8 copy-start.13
  1.5 0.8 copy-start.14
  2.2 0.7 copy-start.15
  2.9 0.7 copy-start.16
  5.0 0.6 copy-start.11
  5.7 33.0 %all-to-all-start = ((bf16[64,8,512]{2,1,0:T(8,128)(2,1)}), bf16[64,8,512]{2,1,0:T(8,128)(2,1)S(1)}, u32[]{:S(2)}, u32[]{:S(2)}) async-start(bf16[64,8,512]{2,1,0:T(8,128)(2,1)} %bitcast.3), calls=%async_computation | async-start | bytes 1048576 | tf_op jit(solution)/shard_map/all_to_all | solution.py:188
  23.0 1.0 copy-start.2
  25.0 15.6 %collective-permute-start.1 = (bf16[672,512]{1,0:T(8,128)(2,1)}, bf16[672,512]{1,0:T(8,128)(2,1)S(1)}, u32[]{:S(2)}, u32[]{:S(2)}) collective-permute-start(bf16[672,512]{1,0:T(8,128)(2,1)} %get-tuple-element.29), channel_id=1, source_target_pairs={{0,64},{64,0},{128,192},{192,128},{256,320},{320,256},{384,448},{4... | collective-permute-start | bytes 2064392 | tf_op jit(solution)/shard_map/ppermute | solution.py:195
  38.7 3.8 %collective-permute-start = (bf16[512,512]{1,0:T(8,128)(2,1)S(1)}, bf16[512,512]{1,0:T(8,128)(2,1)S(1)}, u32[]{:S(2)}, u32[]{:S(2)}) collective-permute-start(bf16[512,512]{1,0:T(8,128)(2,1)S(1)} %bitcast.19), channel_id=1, source_target_pairs={{0,64},{64,0},{128,192},{192,128},{256,320},{320,256},{384,448},{4... | collective-permute-start | bytes 1572872 | tf_op jit(solution)/shard_map/ppermute | solution.py:196
  43.7 0.7 copy-start.9
  93.6 46.3 %copy-start.3 = (bf16[1,1024,224]{1,2,0:T(8,128)(2,1)S(1)}, bf16[1,1024,224]{1,2,0:T(8,128)(2,1)}, u32[]{:S(2)}) copy-start(bf16[1,1024,224]{1,2,0:T(8,128)(2,1)} %param.12) | copy-start | bytes 1376260
  93.6 27.2 %all-to-all-start.2 = ((bf16[8,48,512]{2,1,0:T(8,128)(2,1)}), bf16[8,48,512]{2,1,0:T(8,128)(2,1)S(1)}, u32[]{:S(2)}, u32[]{:S(2)}) async-start(bf16[8,48,512]{2,1,0:T(8,128)(2,1)} %get-tuple-element.33), calls=%async_computation.2 | async-start | bytes 786432 | tf_op jit(solution)/shard_map/all_to_all | solution.py:210
  120.7 19.1 %collective-permute-start.2 = (bf16[384,512]{1,0:T(8,128)(2,1)S(1)}, bf16[384,512]{1,0:T(8,128)(2,1)S(1)}, u32[]{:S(2)}, u32[]{:S(2)}) collective-permute-start(bf16[384,512]{1,0:T(8,128)(2,1)S(1)} %bitcast.28), channel_id=1, source_target_pairs={{0,64},{64,0},{128,192},{192,128},{256,320},{320,256},{384,448},{4... | collective-permute-start | bytes 1179656 | tf_op jit(solution)/shard_map/ppermute | solution.py:215
  141.4 0.9 copy-start.4
  142.3 0.9 copy-start.6
  143.2 0.8 copy-start.8
  144.0 5.4 %copy-start.5 = (bf16[384,1024]{1,0:T(8,128)(2,1)S(1)}, bf16[384,1024]{1,0:T(8,128)(2,1)}, u32[]{:S(2)}) copy-start(bf16[384,1024]{1,0:T(8,128)(2,1)} %copy-done.4) | copy-start | bytes 2359300
  144.0 25.3 %all-to-all-start.3 = ((bf16[64,8,512]{2,1,0:T(8,128)(2,1)}), bf16[64,8,512]{2,1,0:T(8,128)(2,1)S(1)}, u32[]{:S(2)}, u32[]{:S(2)}) async-start(bf16[64,8,512]{2,1,0:T(8,128)(2,1)} %bitcast.31), calls=%async_computation.3 | async-start | bytes 1048576 | tf_op jit(solution)/shard_map/all_to_all | solution.py:225
  149.4 1.1 copy-start.7
  150.5 1.0 copy-start.10
  151.5 17.8 %copy-start.12 = (bf16[512,128]{1,0:T(8,128)(2,1)S(1)}, bf16[512,128]{1,0:T(8,128)(2,1)}, u32[]{:S(2)}) copy-start(bf16[512,128]{1,0:T(8,128)(2,1)} %copy-done.11) | copy-start | bytes 393220

commit v3 on v2

--- a/solution.py
+++ b/solution.py
@@ -19,19 +19,18 @@
     return lax.dot_general(a, b, dims, preferred_element_type=F32)
 
 
-def vmem(count):
-    return [pl.BlockSpec(memory_space=pltpu.VMEM)] * count
-
-
-def call(kernel, outs, *args, scalars=0, scratch=()):
-    specs = [pl.BlockSpec(memory_space=pltpu.SMEM)] * scalars + vmem(len(args) - scalars)
+def call(kernel, outs, *args, scalars=0, far=(), far_in=False, scratch=(), limit=LIMIT):
+    near = pl.BlockSpec(memory_space=pltpu.VMEM)
+    away = pl.BlockSpec(memory_space=pl.ANY)
+    specs = [pl.BlockSpec(memory_space=pltpu.SMEM)] * scalars
+    specs += [away if far_in else near] * (len(args) - scalars)
     return pl.pallas_call(
         kernel,
         out_shape=[jax.ShapeDtypeStruct(shape, dtype) for shape, dtype in outs],
         in_specs=specs,
-        out_specs=vmem(len(outs)),
+        out_specs=[away if i in far else near for i in range(len(outs))],
         scratch_shapes=list(scratch),
-        compiler_params=pltpu.CompilerParams(vmem_limit_bytes=LIMIT),
+        compiler_params=pltpu.CompilerParams(vmem_limit_bytes=limit),
     )(*args)
 
 
@@ -44,7 +43,19 @@
             ref[part * width : (part + 1) * width, :] = mat_ref[:, pl.ds(start, half)]
 
 
-def route_kernel(ids_ref, weight_ref, token_ref, grad_ref, send_ref, mark_ref, scale_ref):
+def route_kernel(
+    ids_in, weight_in, token_in, grad_in, send_out, mark_out, scale_out,
+    ids_ref, weight_ref, token_ref, grad_ref, send_ref, mark_ref, scale_ref, sems,
+):
+    pairs = (
+        (ids_in, ids_ref), (weight_in, weight_ref), (token_in, token_ref), (grad_in, grad_ref),
+        (mark_ref, mark_out), (scale_ref, scale_out), (send_ref, send_out),
+    )
+    copies = [pltpu.make_async_copy(*pair, sems.at[i]) for i, pair in enumerate(pairs)]
+    for copy in copies[:4]:
+        copy.start()
+    copies[0].wait()
+    copies[1].wait()
     picks, tokens = ids_ref.shape
     width = token_ref.shape[1]
     rows = mark_ref.shape[0]
@@ -71,10 +82,17 @@
     scale = jnp.concatenate([scales[0] + scales[1], scales[2] + scales[3]], axis=1).astype(BF16)
     mark_ref[...] = mark
     scale_ref[...] = scale
+    copies[4].start()
+    copies[5].start()
+    copies[2].wait()
+    copies[3].wait()
     twice = lambda ref: jnp.concatenate([ref[...], ref[...]], axis=0)
     send_ref[...] = jnp.zeros_like(send_ref)
     send_ref[:, 0:width] = mm(mark, twice(token_ref)).astype(BF16)
     send_ref[:, side : side + width] = mm(scale, twice(grad_ref)).astype(BF16)
+    copies[6].start()
+    for copy in copies[4:]:
+        copy.wait()
 
 
 def slot_matrix(rows, kept, turned):
@@ -85,7 +103,9 @@
     return (lax.rem(small, sources) * SLOTS + small // sources == large).astype(BF16)
 
 
-def sums_kernel(mine_ref, theirs_ref, own_ref, other_ref, sum_ref, kept_ref):
+def sums_kernel(
+    mine_ref, theirs_ref, own_ref, other_ref, sum_ref, kept_out, kept_ref, sem
+):
     rows, wide = mine_ref.shape
     kept = sum_ref.shape[0]
     side = wide // 2
@@ -94,6 +114,8 @@
     pack = slot_matrix(rows, kept, False)
     mine = mm(pack, mine_ref[...]).astype(BF16)
     kept_ref[...] = mine
+    copy = pltpu.make_async_copy(kept_ref, kept_out, sem)
+    copy.start()
     theirs = mm(pack, theirs_ref[...]).astype(BF16)
     for part, lo in enumerate((0, 0, side)):
         block = slice(part * width, (part + 1) * width)
@@ -101,57 +123,78 @@
             mm(mine[:, lo : lo + width], own_ref[block, :])
             + mm(theirs[:, lo : lo + width], other_ref[block, :])
         ).astype(BF16)
-
-
-def hidden_kernel(sum_ref, hid_ref, dgate_ref, dup_ref):
+    copy.wait()
+
+
+def power_of_two(exponent):
+    left = jnp.abs(exponent)
+    result = jnp.ones_like(exponent)
+    for bit in (64, 32, 16, 8, 4, 2, 1):
+        taken = left >= bit
+        step = jnp.where(exponent >= 0, 2.0**bit, 2.0**-bit)
+        result = jnp.where(taken, result * step, result)
+        left = jnp.where(taken, left - bit, left)
+    return result
+
+
+def hidden_kernel(sum_ref, out_ref):
     half = sum_ref.shape[2] // 3
     total = lambda part: jnp.sum(
         sum_ref[:, :, part * half : (part + 1) * half].astype(F32), axis=0
     )
     gate, up, back = total(0), total(1), total(2)
     sig = jax.nn.sigmoid(gate)
-    hid = (gate * sig * up).astype(BF16)
-    for peer in range(hid_ref.shape[0]):
-        hid_ref[peer] = hid
-    dgate_ref[...] = (back * up * (sig * (1.0 + gate * (1.0 - sig)))).astype(BF16)
-    dup_ref[...] = (back * (gate * sig)).astype(BF16)
-
-
-def rows_kernel(
-    core_ref, own_ref, other_ref, dgates_ref, dups_ref, gate_ref, up_ref, down_ref,
-    send_ref, hid_ref, dgate_ref, dup_ref, out_ref,
+    values = (
+        gate * sig * up,
+        back * up * (sig * (1.0 + gate * (1.0 - sig))),
+        back * (gate * sig),
+    )
+    lane = lax.broadcasted_iota(jnp.int32, (gate.shape[0], 128), 1)
+    exponents = jnp.zeros(lane.shape, F32)
+    for part, value in enumerate(values):
+        value = value.astype(BF16).astype(F32)
+        peak = jnp.max(jnp.abs(value), axis=1, keepdims=True)
+        exponent = jnp.ceil(jnp.log2(jnp.maximum(peak, 2.0**-100))) - 15.0
+        out_ref[:, part * half : (part + 1) * half] = (
+            value * power_of_two(-exponent)
+        ).astype(out_ref.dtype)
+        exponents = jnp.where(lane == part, exponent, exponents)
+    out_ref[:, 3 * half :] = exponents.astype(out_ref.dtype)
+
+
+def products_kernel(
+    all_ref, kept_ref, gate_ref, up_ref, down_ref,
+    send_ref, gate_sum_ref, up_sum_ref, down_sum_ref,
+    hid_ref, dgate_ref, dup_ref, out_ref, rows_ref, sem,
 ):
     kept, hidden = hid_ref.shape
     half = hidden // 2
     width = gate_ref.shape[0]
     side = out_ref.shape[1] // 2
-    block = dgates_ref.shape[0] // 16
-    for ref, which in ((own_ref, core_ref[0]), (other_ref, 1 - core_ref[0])):
-        hid_ref[:, pl.ds(pl.multiple_of(which * half, half), half)] = ref[...]
+    block = all_ref.shape[0] // 16
     for index in range(16):
         chip, core = index // 2, index % 2
-        for ref, piece_ref in ((dgate_ref, dgates_ref), (dup_ref, dups_ref)):
-            ref[chip * block : (chip + 1) * block, core * half : (core + 1) * half] = piece_ref[
-                index * block : (index + 1) * block, :
-            ]
+        lines = slice(index * block, (index + 1) * block)
+        scale = power_of_two(all_ref[lines, 3 * half :].astype(F32))
+        for part, ref in enumerate((hid_ref, dgate_ref, dup_ref)):
+            ref[chip * block : (chip + 1) * block, core * half : (core + 1) * half] = (
+                all_ref[lines, part * half : (part + 1) * half].astype(F32)
+                * scale[:, part : part + 1]
+            ).astype(BF16)
     out_ref[...] = jnp.zeros_like(out_ref)
     out_ref[:, 0:width] = mm(hid_ref[...], down_ref[...], NT).astype(BF16)
     out_ref[:, side : side + width] = (
         mm(dgate_ref[...], gate_ref[...], NT) + mm(dup_ref[...], up_ref[...], NT)
     ).astype(BF16)
-    send_ref[...] = mm(slot_matrix(send_ref.shape[0], kept, True), out_ref[...]).astype(BF16)
-
-
-def weights_kernel(
-    kept_ref, hid_ref, dgate_ref, dup_ref, gate_sum_ref, up_sum_ref, down_sum_ref
-):
-    width = gate_sum_ref.shape[0]
-    side = kept_ref.shape[1] // 2
+    rows_ref[...] = mm(slot_matrix(rows_ref.shape[0], kept, True), out_ref[...]).astype(BF16)
+    copy = pltpu.make_async_copy(rows_ref, send_ref, sem)
+    copy.start()
     token_rows = kept_ref[:, 0:width]
     grad_rows = kept_ref[:, side : side + width]
     gate_sum_ref[...] = mm(token_rows, dgate_ref[...], TN).astype(BF16)
     up_sum_ref[...] = mm(token_rows, dup_ref[...], TN).astype(BF16)
     down_sum_ref[...] = mm(grad_rows, hid_ref[...], TN).astype(BF16)
+    copy.wait()
 
 
 def combine_kernel(back_ref, mark_ref, scale_ref, mixed_ref, token_grad_ref):
@@ -180,10 +223,18 @@
     core = (lax.axis_index("rep") % 2).astype(jnp.int32).reshape(1)
     gate_mat, up_mat, down_mat = w_gate[0], w_up[0], w_down[0].T
 
+    routed = (expert_ids.T, route_weights.T, tokens, grad_out)
     send, mark, scale = call(
         route_kernel,
         [((rows, 2 * side), BF16), ((rows, 2 * count), BF16), ((rows, 2 * count), BF16)],
-        expert_ids.T, route_weights.T, tokens, grad_out,
+        *routed,
+        far=(0, 1, 2),
+        far_in=True,
+        limit=60 * 1024 * 1024,
+        scratch=[pltpu.VMEM(a.shape, a.dtype) for a in routed]
+        + [pltpu.VMEM((rows, 2 * side), BF16)]
+        + [pltpu.VMEM((rows, 2 * count), BF16)] * 2
+        + [pltpu.SemaphoreType.DMA((7,))],
     )
     mine = lax.all_to_all(
         send.reshape(experts, SLOTS, 2 * side), ("node", "local"), 0, 0, tiled=True
@@ -198,36 +249,35 @@
         sums_kernel,
         [((kept, 3 * half), BF16), ((kept, 2 * side), BF16)],
         mine, theirs, own, other,
+        far=(1,),
+        scratch=[pltpu.VMEM((kept, 2 * side), BF16), pltpu.SemaphoreType.DMA(())],
     )
     sums = lax.all_to_all(
         sums.reshape(chips, kept // chips, 3 * half),
         "rep", 0, 0, tiled=True, axis_index_groups=lines,
     )
-    piece = ((kept // chips, half), BF16)
-    hid, dgate, dup = call(
-        hidden_kernel, [((chips,) + piece[0], BF16), piece, piece], sums
-    )
-    hid_own = lax.all_to_all(
-        hid, "rep", 0, 0, tiled=True, axis_index_groups=lines
-    ).reshape(kept, half)
-    dgates = lax.all_gather(dgate, "rep", axis=0, tiled=True)
-    dgates, dup, hid_own = lax.optimization_barrier((dgates, dup, hid_own))
-    hid_other = lax.ppermute(hid_own, "rep", swap)
-    dups = lax.all_gather(dup, "rep", axis=0, tiled=True)
-    matrix = ((kept, hidden), BF16)
-    send_back, hid, dgate, dup = call(
-        rows_kernel,
-        [((rows, 2 * side), BF16), matrix, matrix, matrix],
-        core, hid_own, hid_other, dgates, dups, gate_mat, up_mat, down_mat,
-        scalars=1,
-        scratch=[pltpu.VMEM((kept, 2 * side), BF16)],
+    (piece,) = call(
+        hidden_kernel, [((kept // chips, 3 * half + 128), BF16)], sums
+    )
+    piece = lax.optimization_barrier(piece.astype(jnp.float16))
+    whole = lax.all_gather(piece, "rep", axis=0, tiled=True)
+    whole = lax.optimization_barrier(whole).astype(BF16)
+    matrix = pltpu.VMEM((kept, hidden), BF16)
+    grads = ((width, hidden), BF16)
+    send_back, gate_sum, up_sum, down_sum = call(
+        products_kernel,
+        [((rows, 2 * side), BF16), grads, grads, grads],
+        whole, kept_rows, gate_mat, up_mat, down_mat,
+        far=(0,),
+        scratch=[
+            matrix, matrix, matrix,
+            pltpu.VMEM((kept, 2 * side), BF16),
+            pltpu.VMEM((rows, 2 * side), BF16),
+            pltpu.SemaphoreType.DMA(()),
+        ],
     )
     back = lax.all_to_all(
         send_back.reshape(experts, SLOTS, 2 * side), ("node", "local"), 0, 0, tiled=True
-    )
-    grads = ((width, hidden), BF16)
-    gate_sum, up_sum, down_sum = call(
-        weights_kernel, [grads, grads, grads], kept_rows, hid, dgate, dup
     )
     mixed, token_grad = call(
         combine_kernel,

time: 171 us -> 146 us (0.85)
  waiting for transfers between devices: 29.8 us -> 12.5 us
  starting transfers between devices: 32.3 us -> 21.2 us
  blocking collectives: 88.7 us -> 97.5 us
  local copies, waits for them, and re-layouts: 10.1 us -> 3.94 us
    all_to_all x0 -> x1, blocking collectives: none -> 24.9 us  [shards(): lax.all_to_all(send_back.reshape(experts, SLOTS, 2 * side), ('node', 'loc...]
    all_to_all x2 -> x0, waiting for transfers between devices: 16.1 us -> none  [the longest x1 16.1 us: shards(): lax.all_to_all(send_back.reshape(experts, SLOTS, 2 * side), ('node', 'loc...]
    all_gather x2 -> x1, blocking collectives: 40.4 us -> 24.3 us  [shards(): whole = lax.all_gather(piece, 'rep', axis=0, tiled=True)]
    all_to_all x2 -> x0, starting transfers between devices: 8.93 us -> none  [the longest x1 5.35 us: shards(): lax.all_to_all(send_back.reshape(experts, SLOTS, 2 * side), ('node', 'loc...]
    unnamed x34 -> x16, local copies, waits for them, and re-layouts: 10.1 us -> 3.94 us
    ppermute x1 -> x0, starting transfers between devices: 2.25 us -> none  [shards(): hid_other = lax.ppermute(hid_own, 'rep', swap)]
    pallas_call x7 -> x6, Pallas kernels: 8.51 us -> 9.3 us  [call(): pl.pallas_call(kernel, out_shape=[jax.ShapeDtypeStruct(shape, dtype) for...]
  transfers between devices with their start and end apart: 6 -> 3, of which waited for: 3 -> 2; matrix products, arithmetic and copies ran while one was open for 0% -> 0% of each run, Pallas kernels for 2% -> 0%
where the time goes in v3:
time: 146 us
  blocking collectives  97.5 us (67%)
  starting transfers between devices  21.2 us (15%)
  waiting for transfers between devices  12.5 us (9%)
  Pallas kernels  9.3 us (6%)
  local copies, waits for them, and re-layouts  3.94 us (3%)
    all_to_all x1, blocking collectives, shards(): lax.all_to_all(sums.reshape(chips, kept // chips, 3 * half), 'rep', 0, 0,...  48.2 us
    all_to_all x1, blocking collectives, shards(): lax.all_to_all(send_back.reshape(experts, SLOTS, 2 * side), ('node', 'loc...  24.9 us
    all_gather x1, blocking collectives, shards(): whole = lax.all_gather(piece, 'rep', axis=0, tiled=True)  24.3 us
    all_to_all x1, starting transfers between devices, shards(): lax.all_to_all(send.reshape(experts, SLOTS, 2 * side), ('node', 'local'),...  17.3 us
    all_to_all x1, waiting for transfers between devices, shards(): lax.all_to_all(send.reshape(experts, SLOTS, 2 * side), ('node', 'local'),...  10.6 us
    pallas_call x6, Pallas kernels, call(): pl.pallas_call(kernel, out_shape=[jax.ShapeDtypeStruct(shape, dtype) for...  9.3 us
    unnamed x16, local copies, waits for them, and re-layouts  3.94 us
  transfers between devices with their start and end apart: 3, of which 2 were waited for; matrix products, arithmetic and copies ran while one was open for 0% of the time, Pallas kernels for 0%

profile of v3, /device:TPU:4, one launch (start us, length us, event | category | flops | bytes accessed | tf_op | source)
XLA Modules:
  0.0 145.6 jit_solution(15074082788155141075)
XLA Ops:
  0.6 2.2 %shard_map.110 = (bf16[512,512]{1,0:T(8,128)(2,1)}, bf16[512,128]{1,0:T(8,128)(2,1)}, bf16[512,128]{1,0:T(8,128)(2,1)}) custom-call(s32[4,64]{1,0:T(4,128)} %bitcast.30, bf16[4,64]{1,0:T(4,128)(2,1)} %bitcast.31, bf16[64,224]{1,0:T(8,128)(2,1)} %token_in.1, bf16[64,224]{1,0:T(8,128)(2,1)} %grad_in.1), custom_call_target="tpu_custom_call" | custom-call | tf_op jit(solution)/shard_map/pallas_call | solution.py:27
  2.9 17.3 %all-to-all-start = ((bf16[64,8,512]{2,1,0:T(8,128)(2,1)}), bf16[64,8,512]{2,1,0:T(8,128)(2,1)S(1)}, u32[]{:S(2)}, u32[]{:S(2)}) async-start(bf16[64,8,512]{2,1,0:T(8,128)(2,1)} %bitcast.29), calls=%async_computation | async-start | bytes 1048576 | tf_op jit(solution)/shard_map/all_to_all | solution.py:239
  20.2 0.0 copy-start
  20.2 1.0 copy-done
  21.2 0.0 copy-start.2
  21.2 1.0 copy-done.2
  22.3 0.0 copy-start.4
  22.3 1.0 copy-done.4
  23.3 0.1 shard_map.111
  23.4 1.9 %collective-permute-start.1 = (bf16[672,512]{1,0:T(8,128)(2,1)S(1)}, bf16[672,512]{1,0:T(8,128)(2,1)S(1)}, u32[]{:S(2)}, u32[]{:S(2)}) collective-permute-start(bf16[672,512]{1,0:T(8,128)(2,1)S(1)} %get-tuple-element.20), channel_id=1, source_target_pairs={{0,64},{64,0},{128,192},{192,128},{256,320},{320,256},{384,448},{4... | collective-permute-start | bytes 2064392 | tf_op jit(solution)/shard_map/ppermute | solution.py:246
  25.3 10.6 %all-to-all-done = bf16[64,8,512]{2,1,0:T(8,128)(2,1)S(1)} async-done(((bf16[64,8,512]{2,1,0:T(8,128)(2,1)}), bf16[64,8,512]{2,1,0:T(8,128)(2,1)S(1)}, u32[]{:S(2)}, u32[]{:S(2)}) %all-to-all-start) | async-done | bytes 524320 | tf_op jit(solution)/shard_map/all_to_all | solution.py:239
  35.9 1.9 %collective-permute-start = (bf16[512,512]{1,0:T(8,128)(2,1)S(1)}, bf16[512,512]{1,0:T(8,128)(2,1)S(1)}, u32[]{:S(2)}, u32[]{:S(2)}) collective-permute-start(bf16[512,512]{1,0:T(8,128)(2,1)S(1)} %bitcast.18), channel_id=1, source_target_pairs={{0,64},{64,0},{128,192},{192,128},{256,320},{320,256},{384,448},{4... | collective-permute-start | bytes 1572872 | tf_op jit(solution)/shard_map/ppermute | solution.py:247
  37.8 0.0 collective-permute-done.1.other_ref
  37.8 1.9 %collective-permute-done.theirs_ref = bf16[512,512]{1,0:T(8,128)(2,1)S(1)} collective-permute-done((bf16[512,512]{1,0:T(8,128)(2,1)S(1)}, bf16[512,512]{1,0:T(8,128)(2,1)S(1)}, u32[]{:S(2)}, u32[]{:S(2)}) %collective-permute-start) | collective-permute-done | bytes 524320 | tf_op jit(solution)/shard_map/ppermute | solution.py:247
  39.7 1.6 %shard_map.112 = (bf16[384,1536]{1,0:T(8,128)(2,1)S(1)}, bf16[384,512]{1,0:T(8,128)(2,1)S(1)}) custom-call(bf16[512,512]{1,0:T(8,128)(2,1)S(1)} %bitcast.19, bf16[512,512]{1,0:T(8,128)(2,1)S(1)} %collective-permute-done.theirs_ref, bf16[672,512]{1,0:T(8,128)(2,1)S(1)} %get-tuple-element.19.own_ref, bf16[672,512]{1,0:T(8,128)(2,1)S(1)} %collective-permute-done.1.other_ref), custom_call_target="tpu_custom_call" | custom-call | tf_op jit(solution)/shard_map/pallas_call | solution.py:27
  41.3 48.2 %all_to_all.15.sum_ref = bf16[8,48,1536]{2,1,0:T(8,128)(2,1)S(1)} all-to-all(bf16[8,48,1536]{2,1,0:T(8,128)(2,1)S(1)} %bitcast.27), channel_id=1, replica_groups={{0,128,256,384,512,640,768,896},{64,192,320,448,576,704,832,960},{1,129..., dimensions={0} | all-to-all | bytes 2359296 | tf_op jit(solution)/shard_map/all_to_all | solution.py:255
  89.6 0.4 shard_map.113
  90.0 24.3 %all-gather.1 = f16[768,1664]{1,0:T(8,128)(2,1)S(1)} all-gather(f16[48,1664]{1,0:T(8,128)(2,1)S(1)} %convert_element_type.6), channel_id=1, replica_groups=mesh['rep'=16,'node'=8,'local'=8] {'rep'}, dimensions={0}, use_global_device_ids=true | all-gather | bytes 2715648 | tf_op jit(solution)/shard_map/all_gather | solution.py:263
  114.3 0.0 copy-start.1
  114.3 0.0 copy-start.3
  114.3 0.0 copy-start.5
  114.3 0.4 convert_element_type.7.all_ref
  114.7 0.6 copy-done.1
  115.3 0.1 copy-done.3
  115.4 0.1 copy-done.5
  115.6 0.0 copy-start.6
  115.6 0.0 copy-start.7
  115.6 4.1 %shard_map.114 = (bf16[512,512]{1,0:T(8,128)(2,1)S(1)}, bf16[224,1024]{1,0:T(8,128)(2,1)}, bf16[224,1024]{1,0:T(8,128)(2,1)}, bf16[224,1024]{1,0:T(8,128)(2,1)}) custom-call(bf16[768,1664]{1,0:T(8,128)(2,1)S(1)} %convert_element_type.7.all_ref, bf16[384,512]{1,0:T(8,128)(2,1)S(1)} %get-tuple-element.22.kept_ref, bf16[224,1024]{1,0:T(8,128)(2,1)S(1)} %bitcast.22, ...), custom_call_target="tpu_custom_call" | custom-call | tf_op jit(solution)/shard_map/pallas_call | solution.py:27
  119.7 24.9 %all_to_all.16 = bf16[64,8,512]{2,1,0:T(8,128)(2,1)S(1)} all-to-all(bf16[64,8,512]{2,1,0:T(8,128)(2,1)S(1)} %bitcast.28), channel_id=1, replica_groups=mesh['rep'=16,'node'=8,'local'=8] {'node','local'}, dimensions={0} | all-to-all | bytes 1048576 | tf_op jit(solution)/shard_map/all_to_all | solution.py:279
  144.7 0.0 copy-done.6
  144.7 0.0 copy-done.7
  144.7 0.9 shard_map.115
  (1 shorter events, 0.0 us)
Async XLA Ops:
  2.9 33.0 %all-to-all-start = ((bf16[64,8,512]{2,1,0:T(8,128)(2,1)}), bf16[64,8,512]{2,1,0:T(8,128)(2,1)S(1)}, u32[]{:S(2)}, u32[]{:S(2)}) async-start(bf16[64,8,512]{2,1,0:T(8,128)(2,1)} %bitcast.29), calls=%async_computation | async-start | bytes 1048576 | tf_op jit(solution)/shard_map/all_to_all | solution.py:239
  20.2 1.0 copy-start
  21.2 1.0 copy-start.2
  22.3 1.0 copy-start.4
  23.4 14.4 %collective-permute-start.1 = (bf16[672,512]{1,0:T(8,128)(2,1)S(1)}, bf16[672,512]{1,0:T(8,128)(2,1)S(1)}, u32[]{:S(2)}, u32[]{:S(2)}) collective-permute-start(bf16[672,512]{1,0:T(8,128)(2,1)S(1)} %get-tuple-element.20), channel_id=1, source_target_pairs={{0,64},{64,0},{128,192},{192,128},{256,320},{320,256},{384,448},{4... | collective-permute-start | bytes 2064392 | tf_op jit(solution)/shard_map/ppermute | solution.py:246
  35.9 3.8 %collective-permute-start = (bf16[512,512]{1,0:T(8,128)(2,1)S(1)}, bf16[512,512]{1,0:T(8,128)(2,1)S(1)}, u32[]{:S(2)}, u32[]{:S(2)}) collective-permute-start(bf16[512,512]{1,0:T(8,128)(2,1)S(1)} %bitcast.18), channel_id=1, source_target_pairs={{0,64},{64,0},{128,192},{192,128},{256,320},{320,256},{384,448},{4... | collective-permute-start | bytes 1572872 | tf_op jit(solution)/shard_map/ppermute | solution.py:247
  114.3 1.0 copy-start.1
  114.3 1.2 copy-start.3
  114.3 1.3 copy-start.5
  115.6 29.1 %copy-start.6 = (bf16[512,128]{1,0:T(8,128)(2,1)S(1)}, bf16[512,128]{1,0:T(8,128)(2,1)}, u32[]{:S(2)}) copy-start(bf16[512,128]{1,0:T(8,128)(2,1)} %get-tuple-element.24.mark_ref) | copy-start | bytes 393220
  115.6 29.1 %copy-start.7 = (bf16[512,128]{1,0:T(8,128)(2,1)S(1)}, bf16[512,128]{1,0:T(8,128)(2,1)}, u32[]{:S(2)}) copy-start(bf16[512,128]{1,0:T(8,128)(2,1)} %get-tuple-element.25.scale_ref) | copy-start | bytes 393220

commit v4 on v3

--- a/solution.py
+++ b/solution.py
@@ -58,16 +58,15 @@
     copies[1].wait()
     picks, tokens = ids_ref.shape
     width = token_ref.shape[1]
-    rows = mark_ref.shape[0]
-    experts = rows // SLOTS
-    side = send_ref.shape[1] // 2
+    kept = mark_ref.shape[0]
+    experts = send_ref.shape[0] // SLOTS
     row_i = lax.broadcasted_iota(jnp.int32, (tokens, tokens), 0)
     col_i = lax.broadcasted_iota(jnp.int32, (tokens, tokens), 1)
     earlier = (row_i < col_i).astype(F32)
     ids = ids_ref[...].astype(F32)
     weights = weight_ref[...].astype(F32)
     expert_i = lax.broadcasted_iota(jnp.int32, (experts, tokens), 0).astype(F32)
-    row_all = lax.broadcasted_iota(jnp.int32, (rows, tokens), 0).astype(F32)
+    row_all = lax.broadcasted_iota(jnp.int32, (kept, tokens), 0).astype(F32)
     before = jnp.zeros((experts, 1), F32)
     marks, scales = [], []
     for pick in range(picks):
@@ -75,7 +74,7 @@
         count = mm(hit, earlier) + before
         slot = jnp.sum(hit * count, axis=0, keepdims=True)
         before = before + jnp.sum(hit, axis=1, keepdims=True)
-        found = row_all == ids[pick : pick + 1, :] * SLOTS + slot
+        found = row_all == slot * experts + ids[pick : pick + 1, :]
         marks.append(jnp.where(found, 1.0, 0.0))
         scales.append(jnp.where(found, weights[pick : pick + 1, :], 0.0))
     mark = jnp.concatenate([marks[0] + marks[1], marks[2] + marks[3]], axis=1).astype(BF16)
@@ -87,41 +86,78 @@
     copies[2].wait()
     copies[3].wait()
     twice = lambda ref: jnp.concatenate([ref[...], ref[...]], axis=0)
-    send_ref[...] = jnp.zeros_like(send_ref)
-    send_ref[:, 0:width] = mm(mark, twice(token_ref)).astype(BF16)
-    send_ref[:, side : side + width] = mm(scale, twice(grad_ref)).astype(BF16)
+    pack_rows(
+        mm(mark, twice(token_ref)).astype(BF16),
+        mm(scale, twice(grad_ref)).astype(BF16),
+        send_ref,
+    )
     copies[6].start()
     for copy in copies[4:]:
         copy.wait()
 
 
+def one_hot(rows, places, turned):
+    shape = (rows, places.shape[1]) if turned else (places.shape[0], rows)
+    return (lax.broadcasted_iota(jnp.int32, shape, 0 if turned else 1) == places).astype(BF16)
+
+
 def slot_matrix(rows, kept, turned):
     sources = rows // SLOTS
-    shape = (rows, kept) if turned else (kept, rows)
-    small = lax.broadcasted_iota(jnp.int32, shape, 1 if turned else 0)
-    large = lax.broadcasted_iota(jnp.int32, shape, 0 if turned else 1)
-    return (lax.rem(small, sources) * SLOTS + small // sources == large).astype(BF16)
+    index = lax.broadcasted_iota(jnp.int32, (1, kept) if turned else (kept, 1), int(turned))
+    return one_hot(rows, lax.rem(index, sources) * SLOTS + index // sources, turned)
+
+
+def spare_matrix(rows, turned):
+    sources = rows // SLOTS
+    shape = (1, sources) if turned else (sources, 1)
+    index = lax.broadcasted_iota(jnp.int32, shape, int(turned))
+    return one_hot(rows, index * SLOTS + SLOTS - 2, turned)
+
+
+def pack_rows(first, second, sent_ref):
+    rows, lanes = sent_ref.shape
+    kept, width = first.shape
+    sources = rows // SLOTS
+    cut = lanes - width
+    wide = jnp.concatenate([first, second[:, :cut]], axis=1)
+    spare = jnp.concatenate(
+        [second[i : i + sources, cut:] for i in range(0, kept, sources)], axis=1
+    )
+    sent_ref[...] = (
+        mm(slot_matrix(rows, kept, True), wide) + mm(spare_matrix(rows, True), spare)
+    ).astype(BF16)
+
+
+def unpack_rows(sent, kept, width):
+    rows, lanes = sent.shape
+    sources = rows // SLOTS
+    rest = 2 * width - lanes
+    wide = mm(slot_matrix(rows, kept, False), sent).astype(BF16)
+    spare = mm(spare_matrix(rows, False), sent).astype(BF16)
+    tail = jnp.concatenate(
+        [spare[:, i * rest : (i + 1) * rest] for i in range(kept // sources)], axis=0
+    )
+    return wide[:, :width], jnp.concatenate([wide[:, width:], tail], axis=1)
 
 
 def sums_kernel(
     mine_ref, theirs_ref, own_ref, other_ref, sum_ref, kept_out, kept_ref, sem
 ):
-    rows, wide = mine_ref.shape
     kept = sum_ref.shape[0]
-    side = wide // 2
     half = own_ref.shape[1]
     width = own_ref.shape[0] // 3
-    pack = slot_matrix(rows, kept, False)
-    mine = mm(pack, mine_ref[...]).astype(BF16)
-    kept_ref[...] = mine
+    side = kept_ref.shape[1] // 2
+    mine = unpack_rows(mine_ref[...], kept, width)
+    kept_ref[...] = jnp.zeros_like(kept_ref)
+    kept_ref[:, 0:width] = mine[0]
+    kept_ref[:, side : side + width] = mine[1]
     copy = pltpu.make_async_copy(kept_ref, kept_out, sem)
     copy.start()
-    theirs = mm(pack, theirs_ref[...]).astype(BF16)
-    for part, lo in enumerate((0, 0, side)):
+    theirs = unpack_rows(theirs_ref[...], kept, width)
+    for part, which in enumerate((0, 0, 1)):
         block = slice(part * width, (part + 1) * width)
         sum_ref[:, part * half : (part + 1) * half] = (
-            mm(mine[:, lo : lo + width], own_ref[block, :])
-            + mm(theirs[:, lo : lo + width], other_ref[block, :])
+            mm(mine[which], own_ref[block, :]) + mm(theirs[which], other_ref[block, :])
         ).astype(BF16)
     copy.wait()
 
@@ -165,12 +201,12 @@
 def products_kernel(
     all_ref, kept_ref, gate_ref, up_ref, down_ref,
     send_ref, gate_sum_ref, up_sum_ref, down_sum_ref,
-    hid_ref, dgate_ref, dup_ref, out_ref, rows_ref, sem,
+    hid_ref, dgate_ref, dup_ref, rows_ref, sem,
 ):
     kept, hidden = hid_ref.shape
     half = hidden // 2
     width = gate_ref.shape[0]
-    side = out_ref.shape[1] // 2
+    side = kept_ref.shape[1] // 2
     block = all_ref.shape[0] // 16
     for index in range(16):
         chip, core = index // 2, index % 2
@@ -181,12 +217,11 @@
                 all_ref[lines, part * half : (part + 1) * half].astype(F32)
                 * scale[:, part : part + 1]
             ).astype(BF16)
-    out_ref[...] = jnp.zeros_like(out_ref)
-    out_ref[:, 0:width] = mm(hid_ref[...], down_ref[...], NT).astype(BF16)
-    out_ref[:, side : side + width] = (
+    out_rows = mm(hid_ref[...], down_ref[...], NT).astype(BF16)
+    back_rows = (
         mm(dgate_ref[...], gate_ref[...], NT) + mm(dup_ref[...], up_ref[...], NT)
     ).astype(BF16)
-    rows_ref[...] = mm(slot_matrix(rows_ref.shape[0], kept, True), out_ref[...]).astype(BF16)
+    pack_rows(out_rows, back_rows, rows_ref)
     copy = pltpu.make_async_copy(rows_ref, send_ref, sem)
     copy.start()
     token_rows = kept_ref[:, 0:width]
@@ -199,9 +234,9 @@
 
 def combine_kernel(back_ref, mark_ref, scale_ref, mixed_ref, token_grad_ref):
     tokens, width = mixed_ref.shape
-    side = back_ref.shape[1] // 2
-    for ref, marks, lo in ((mixed_ref, scale_ref, 0), (token_grad_ref, mark_ref, side)):
-        parts = mm(marks[...], back_ref[:, lo : lo + width], TN).astype(BF16).astype(F32)
+    back = unpack_rows(back_ref[...], mark_ref.shape[0], width)
+    for ref, marks, values in zip((mixed_ref, token_grad_ref), (scale_ref, mark_ref), back):
+        parts = mm(marks[...], values, TN).astype(BF16).astype(F32)
         ref[...] = (parts[0:tokens] + parts[tokens:]).astype(BF16)
 
 
@@ -217,6 +252,7 @@
     depth = min(mean_count + max(mean_count // 2, 1), node_hits)
     kept = experts * depth
     rows = experts * SLOTS
+    lanes = 2 * width * depth // (depth + 1)
     lines = [list(range(c, rep, 2)) for c in range(2)]
     chips = rep // 2
     swap = [(i, i ^ 1) for i in range(rep)]
@@ -226,19 +262,19 @@
     routed = (expert_ids.T, route_weights.T, tokens, grad_out)
     send, mark, scale = call(
         route_kernel,
-        [((rows, 2 * side), BF16), ((rows, 2 * count), BF16), ((rows, 2 * count), BF16)],
+        [((rows, lanes), BF16), ((kept, 2 * count), BF16), ((kept, 2 * count), BF16)],
         *routed,
         far=(0, 1, 2),
         far_in=True,
         limit=60 * 1024 * 1024,
         scratch=[pltpu.VMEM(a.shape, a.dtype) for a in routed]
-        + [pltpu.VMEM((rows, 2 * side), BF16)]
-        + [pltpu.VMEM((rows, 2 * count), BF16)] * 2
+        + [pltpu.VMEM((rows, lanes), BF16)]
+        + [pltpu.VMEM((kept, 2 * count), BF16)] * 2
         + [pltpu.SemaphoreType.DMA((7,))],
     )
     mine = lax.all_to_all(
-        send.reshape(experts, SLOTS, 2 * side), ("node", "local"), 0, 0, tiled=True
-    ).reshape(rows, 2 * side)
+        send.reshape(experts, SLOTS, lanes), ("node", "local"), 0, 0, tiled=True
+    ).reshape(rows, lanes)
     packed = ((3 * width, half), BF16)
     own, give = call(
         pack_kernel, [packed, packed], core, gate_mat, up_mat, down_mat, scalars=1
@@ -266,23 +302,22 @@
     grads = ((width, hidden), BF16)
     send_back, gate_sum, up_sum, down_sum = call(
         products_kernel,
-        [((rows, 2 * side), BF16), grads, grads, grads],
+        [((rows, lanes), BF16), grads, grads, grads],
         whole, kept_rows, gate_mat, up_mat, down_mat,
         far=(0,),
         scratch=[
             matrix, matrix, matrix,
-            pltpu.VMEM((kept, 2 * side), BF16),
-            pltpu.VMEM((rows, 2 * side), BF16),
+            pltpu.VMEM((rows, lanes), BF16),
             pltpu.SemaphoreType.DMA(()),
         ],
     )
     back = lax.all_to_all(
-        send_back.reshape(experts, SLOTS, 2 * side), ("node", "local"), 0, 0, tiled=True
+        send_back.reshape(experts, SLOTS, lanes), ("node", "local"), 0, 0, tiled=True
     )
     mixed, token_grad = call(
         combine_kernel,
         [(tokens.shape, BF16), (tokens.shape, BF16)],
-        back.reshape(rows, 2 * side), mark, scale,
+        back.reshape(rows, lanes), mark, scale,
     )
     return (mixed, token_grad, gate_sum[None], up_sum[None], down_sum.T[None])
 

time: 146 us -> 142 us (0.973)
  blocking collectives: 97.5 us -> 93.7 us
  waiting for transfers between devices: 12.5 us -> 10.4 us
  Pallas kernels: 9.3 us -> 10.8 us
    all_to_all x1, blocking collectives: 24.9 us -> 22.1 us  [shards(): lax.all_to_all(send_back.reshape(experts, SLOTS, lanes), ('node', 'local'...]
    all_to_all x1, waiting for transfers between devices: 10.6 us -> 8.76 us  [shards(): lax.all_to_all(send.reshape(experts, SLOTS, lanes), ('node', 'local'), 0,...]
    pallas_call x6, Pallas kernels: 9.3 us -> 10.8 us  [call(): pl.pallas_call(kernel, out_shape=[jax.ShapeDtypeStruct(shape, dtype) for...]
where the time goes in v4:
time: 142 us; the launch traced here: 141 us
  blocking collectives  93.7 us (66%)
  starting transfers between devices  21.2 us (15%)
  Pallas kernels  10.8 us (8%)
  waiting for transfers between devices  10.4 us (7%)
  local copies, waits for them, and re-layouts  3.94 us (3%)
    all_to_all x1, blocking collectives, shards(): lax.all_to_all(sums.reshape(chips, kept // chips, 3 * half), 'rep', 0, 0,...  47.3 us
    all_gather x1, blocking collectives, shards(): whole = lax.all_gather(piece, 'rep', axis=0, tiled=True)  24.3 us
    all_to_all x1, blocking collectives, shards(): lax.all_to_all(send_back.reshape(experts, SLOTS, lanes), ('node', 'local'...  22.1 us
    all_to_all x1, starting transfers between devices, shards(): lax.all_to_all(send.reshape(experts, SLOTS, lanes), ('node', 'local'), 0,...  17.3 us
    pallas_call x6, Pallas kernels, call(): pl.pallas_call(kernel, out_shape=[jax.ShapeDtypeStruct(shape, dtype) for...  10.8 us
    all_to_all x1, waiting for transfers between devices, shards(): lax.all_to_all(send.reshape(experts, SLOTS, lanes), ('node', 'local'), 0,...  8.76 us
    unnamed x16, local copies, waits for them, and re-layouts  3.94 us
  transfers between devices with their start and end apart: 3, of which 2 were waited for; matrix products, arithmetic and copies ran while one was open for 0% of the time, Pallas kernels for 0%

profile of v4, /device:TPU:4, one launch (start us, length us, event | category | flops | bytes accessed | tf_op | source)
XLA Modules:
  0.0 141.2 jit_solution(10718207175152452586)
XLA Ops:
  0.6 2.7 %shard_map.110 = (bf16[512,384]{1,0:T(8,128)(2,1)}, bf16[384,128]{1,0:T(8,128)(2,1)}, bf16[384,128]{1,0:T(8,128)(2,1)}) custom-call(s32[4,64]{1,0:T(4,128)} %bitcast.30, bf16[4,64]{1,0:T(4,128)(2,1)} %bitcast.31, bf16[64,224]{1,0:T(8,128)(2,1)} %token_in.1, bf16[64,224]{1,0:T(8,128)(2,1)} %grad_in.1), custom_call_target="tpu_custom_call" | custom-call | tf_op jit(solution)/shard_map/pallas_call | solution.py:27
  3.4 17.3 %all-to-all-start = ((bf16[64,8,384]{2,1,0:T(8,128)(2,1)}), bf16[64,8,384]{2,1,0:T(8,128)(2,1)S(1)}, u32[]{:S(2)}, u32[]{:S(2)}) async-start(bf16[64,8,384]{2,1,0:T(8,128)(2,1)} %bitcast.29), calls=%async_computation | async-start | bytes 786432 | tf_op jit(solution)/shard_map/all_to_all | solution.py:275
  20.7 0.0 copy-start
  20.7 1.0 copy-done
  21.7 0.0 copy-start.2
  21.7 1.0 copy-done.2
  22.7 0.0 copy-start.4
  22.8 1.0 copy-done.4
  23.8 0.1 shard_map.111
  23.9 1.9 %collective-permute-start.1 = (bf16[672,512]{1,0:T(8,128)(2,1)S(1)}, bf16[672,512]{1,0:T(8,128)(2,1)S(1)}, u32[]{:S(2)}, u32[]{:S(2)}) collective-permute-start(bf16[672,512]{1,0:T(8,128)(2,1)S(1)} %get-tuple-element.20), channel_id=1, source_target_pairs={{0,64},{64,0},{128,192},{192,128},{256,320},{320,256},{384,448},{4... | collective-permute-start | bytes 2064392 | tf_op jit(solution)/shard_map/ppermute | solution.py:282
  25.8 8.8 %all-to-all-done = bf16[64,8,384]{2,1,0:T(8,128)(2,1)S(1)} async-done(((bf16[64,8,384]{2,1,0:T(8,128)(2,1)}), bf16[64,8,384]{2,1,0:T(8,128)(2,1)S(1)}, u32[]{:S(2)}, u32[]{:S(2)}) %all-to-all-start) | async-done | bytes 393248 | tf_op jit(solution)/shard_map/all_to_all | solution.py:275
  34.6 1.9 %collective-permute-start = (bf16[512,384]{1,0:T(8,128)(2,1)S(1)}, bf16[512,384]{1,0:T(8,128)(2,1)S(1)}, u32[]{:S(2)}, u32[]{:S(2)}) collective-permute-start(bf16[512,384]{1,0:T(8,128)(2,1)S(1)} %bitcast.25), channel_id=1, source_target_pairs={{0,64},{64,0},{128,192},{192,128},{256,320},{320,256},{384,448},{4... | collective-permute-start | bytes 1179656 | tf_op jit(solution)/shard_map/ppermute | solution.py:283
  36.5 0.0 collective-permute-done.1.other_ref
  36.5 1.7 %collective-permute-done.theirs_ref = bf16[512,384]{1,0:T(8,128)(2,1)S(1)} collective-permute-done((bf16[512,384]{1,0:T(8,128)(2,1)S(1)}, bf16[512,384]{1,0:T(8,128)(2,1)S(1)}, u32[]{:S(2)}, u32[]{:S(2)}) %collective-permute-start) | collective-permute-done | bytes 393248 | tf_op jit(solution)/shard_map/ppermute | solution.py:283
  38.2 1.8 %shard_map.112 = (bf16[384,1536]{1,0:T(8,128)(2,1)S(1)}, bf16[384,512]{1,0:T(8,128)(2,1)S(1)}) custom-call(bf16[512,384]{1,0:T(8,128)(2,1)S(1)} %bitcast.26, bf16[512,384]{1,0:T(8,128)(2,1)S(1)} %collective-permute-done.theirs_ref, bf16[672,512]{1,0:T(8,128)(2,1)S(1)} %get-tuple-element.19.own_ref, bf16[672,512]{1,0:T(8,128)(2,1)S(1)} %collective-permute-done.1.other_ref), custom_call_target="tpu_custom_call" | custom-call | tf_op jit(solution)/shard_map/pallas_call | solution.py:27
  40.0 47.3 %all_to_all.15.sum_ref = bf16[8,48,1536]{2,1,0:T(8,128)(2,1)S(1)} all-to-all(bf16[8,48,1536]{2,1,0:T(8,128)(2,1)S(1)} %bitcast.27), channel_id=1, replica_groups={{0,128,256,384,512,640,768,896},{64,192,320,448,576,704,832,960},{1,129..., dimensions={0} | all-to-all | bytes 2359296 | tf_op jit(solution)/shard_map/all_to_all | solution.py:291
  87.3 0.4 shard_map.113
  87.7 24.3 %all-gather.1 = f16[768,1664]{1,0:T(8,128)(2,1)S(1)} all-gather(f16[48,1664]{1,0:T(8,128)(2,1)S(1)} %convert_element_type.6), channel_id=1, replica_groups=mesh['rep'=16,'node'=8,'local'=8] {'rep'}, dimensions={0}, use_global_device_ids=true | all-gather | bytes 2715648 | tf_op jit(solution)/shard_map/all_gather | solution.py:299
  112.0 0.0 copy-start.1
  112.0 0.0 copy-start.3
  112.0 0.0 copy-start.5
  112.1 0.4 convert_element_type.7.all_ref
  112.5 0.6 copy-done.1
  113.1 0.1 copy-done.3
  113.2 0.1 copy-done.5
  113.3 0.0 copy-start.6
  113.3 0.0 copy-start.7
  113.3 4.4 %shard_map.114 = (bf16[512,384]{1,0:T(8,128)(2,1)S(1)}, bf16[224,1024]{1,0:T(8,128)(2,1)}, bf16[224,1024]{1,0:T(8,128)(2,1)}, bf16[224,1024]{1,0:T(8,128)(2,1)}) custom-call(bf16[768,1664]{1,0:T(8,128)(2,1)S(1)} %convert_element_type.7.all_ref, bf16[384,512]{1,0:T(8,128)(2,1)S(1)} %get-tuple-element.22.kept_ref, bf16[224,1024]{1,0:T(8,128)(2,1)S(1)} %bitcast.19, ...), custom_call_target="tpu_custom_call" | custom-call | tf_op jit(solution)/shard_map/pallas_call | solution.py:27
  117.8 22.1 %all_to_all.16 = bf16[64,8,384]{2,1,0:T(8,128)(2,1)S(1)} all-to-all(bf16[64,8,384]{2,1,0:T(8,128)(2,1)S(1)} %bitcast.28), channel_id=1, replica_groups=mesh['rep'=16,'node'=8,'local'=8] {'node','local'}, dimensions={0} | all-to-all | bytes 786432 | tf_op jit(solution)/shard_map/all_to_all | solution.py:314
  139.8 0.0 copy-done.6
  139.8 0.0 copy-done.7
  139.8 1.4 shard_map.115
  (1 shorter events, 0.0 us)
Async XLA Ops:
  3.4 31.2 %all-to-all-start = ((bf16[64,8,384]{2,1,0:T(8,128)(2,1)}), bf16[64,8,384]{2,1,0:T(8,128)(2,1)S(1)}, u32[]{:S(2)}, u32[]{:S(2)}) async-start(bf16[64,8,384]{2,1,0:T(8,128)(2,1)} %bitcast.29), calls=%async_computation | async-start | bytes 786432 | tf_op jit(solution)/shard_map/all_to_all | solution.py:275
  20.7 1.0 copy-start
  21.7 1.0 copy-start.2
  22.7 1.0 copy-start.4
  23.9 12.6 %collective-permute-start.1 = (bf16[672,512]{1,0:T(8,128)(2,1)S(1)}, bf16[672,512]{1,0:T(8,128)(2,1)S(1)}, u32[]{:S(2)}, u32[]{:S(2)}) collective-permute-start(bf16[672,512]{1,0:T(8,128)(2,1)S(1)} %get-tuple-element.20), channel_id=1, source_target_pairs={{0,64},{64,0},{128,192},{192,128},{256,320},{320,256},{384,448},{4... | collective-permute-start | bytes 2064392 | tf_op jit(solution)/shard_map/ppermute | solution.py:282
  34.6 3.6 %collective-permute-start = (bf16[512,384]{1,0:T(8,128)(2,1)S(1)}, bf16[512,384]{1,0:T(8,128)(2,1)S(1)}, u32[]{:S(2)}, u32[]{:S(2)}) collective-permute-start(bf16[512,384]{1,0:T(8,128)(2,1)S(1)} %bitcast.25), channel_id=1, source_target_pairs={{0,64},{64,0},{128,192},{192,128},{256,320},{320,256},{384,448},{4... | collective-permute-start | bytes 1179656 | tf_op jit(solution)/shard_map/ppermute | solution.py:283
  112.0 1.0 copy-start.1
  112.0 1.2 copy-start.3
  112.0 1.3 copy-start.5
  113.3 26.5 %copy-start.6 = (bf16[384,128]{1,0:T(8,128)(2,1)S(1)}, bf16[384,128]{1,0:T(8,128)(2,1)}, u32[]{:S(2)}) copy-start(bf16[384,128]{1,0:T(8,128)(2,1)} %get-tuple-element.24.mark_ref) | copy-start | bytes 294916
  113.3 26.5 %copy-start.7 = (bf16[384,128]{1,0:T(8,128)(2,1)S(1)}, bf16[384,128]{1,0:T(8,128)(2,1)}, u32[]{:S(2)}) copy-start(bf16[384,128]{1,0:T(8,128)(2,1)} %get-tuple-element.25.scale_ref) | copy-start | bytes 294916

commit v5 on v4

--- a/solution.py
+++ b/solution.py
@@ -19,11 +19,11 @@
     return lax.dot_general(a, b, dims, preferred_element_type=F32)
 
 
-def call(kernel, outs, *args, scalars=0, far=(), far_in=False, scratch=(), limit=LIMIT):
+def call(kernel, outs, *args, scalars=0, far=(), far_in=(), scratch=(), limit=LIMIT):
     near = pl.BlockSpec(memory_space=pltpu.VMEM)
     away = pl.BlockSpec(memory_space=pl.ANY)
     specs = [pl.BlockSpec(memory_space=pltpu.SMEM)] * scalars
-    specs += [away if far_in else near] * (len(args) - scalars)
+    specs += [away if i in far_in else near for i in range(scalars, len(args))]
     return pl.pallas_call(
         kernel,
         out_shape=[jax.ShapeDtypeStruct(shape, dtype) for shape, dtype in outs],
@@ -49,9 +49,18 @@
 ):
     pairs = (
         (ids_in, ids_ref), (weight_in, weight_ref), (token_in, token_ref), (grad_in, grad_ref),
-        (mark_ref, mark_out), (scale_ref, scale_out), (send_ref, send_out),
+        (mark_ref, mark_out), (scale_ref, scale_out),
     )
     copies = [pltpu.make_async_copy(*pair, sems.at[i]) for i, pair in enumerate(pairs)]
+
+    def leave(lines):
+        copies.append(
+            pltpu.make_async_copy(
+                send_ref.at[lines, :], send_out.at[lines, :], sems.at[len(copies)]
+            )
+        )
+        copies[-1].start()
+
     for copy in copies[:4]:
         copy.start()
     copies[0].wait()
@@ -67,11 +76,12 @@
     weights = weight_ref[...].astype(F32)
     expert_i = lax.broadcasted_iota(jnp.int32, (experts, tokens), 0).astype(F32)
     row_all = lax.broadcasted_iota(jnp.int32, (kept, tokens), 0).astype(F32)
+    hits = [(expert_i == ids[pick : pick + 1, :]).astype(F32) for pick in range(picks)]
+    counts = mm(jnp.concatenate(hits, axis=0).astype(BF16), earlier.astype(BF16))
     before = jnp.zeros((experts, 1), F32)
     marks, scales = [], []
-    for pick in range(picks):
-        hit = (expert_i == ids[pick : pick + 1, :]).astype(F32)
-        count = mm(hit, earlier) + before
+    for pick, hit in enumerate(hits):
+        count = counts[pick * experts : (pick + 1) * experts] + before
         slot = jnp.sum(hit * count, axis=0, keepdims=True)
         before = before + jnp.sum(hit, axis=1, keepdims=True)
         found = row_all == slot * experts + ids[pick : pick + 1, :]
@@ -90,8 +100,9 @@
         mm(mark, twice(token_ref)).astype(BF16),
         mm(scale, twice(grad_ref)).astype(BF16),
         send_ref,
-    )
-    copies[6].start()
+        4,
+        leave,
+    )
     for copy in copies[4:]:
         copy.wait()
 
@@ -101,20 +112,20 @@
     return (lax.broadcasted_iota(jnp.int32, shape, 0 if turned else 1) == places).astype(BF16)
 
 
-def slot_matrix(rows, kept, turned):
+def slot_places(rows, kept, shape=None):
     sources = rows // SLOTS
-    index = lax.broadcasted_iota(jnp.int32, (1, kept) if turned else (kept, 1), int(turned))
-    return one_hot(rows, lax.rem(index, sources) * SLOTS + index // sources, turned)
-
-
-def spare_matrix(rows, turned):
-    sources = rows // SLOTS
-    shape = (1, sources) if turned else (sources, 1)
-    index = lax.broadcasted_iota(jnp.int32, shape, int(turned))
-    return one_hot(rows, index * SLOTS + SLOTS - 2, turned)
-
-
-def pack_rows(first, second, sent_ref):
+    shape = shape or (1, kept)
+    index = lax.broadcasted_iota(jnp.int32, shape, 0 if shape[1] == 1 else 1)
+    return lax.rem(index, sources) * SLOTS + index // sources
+
+
+def spare_places(rows, shape=None):
+    shape = shape or (1, rows // SLOTS)
+    index = lax.broadcasted_iota(jnp.int32, shape, 0 if shape[1] == 1 else 1)
+    return index * SLOTS + SLOTS - 2
+
+
+def pack_rows(first, second, sent_ref, blocks, leave):
     rows, lanes = sent_ref.shape
     kept, width = first.shape
     sources = rows // SLOTS
@@ -123,43 +134,58 @@
     spare = jnp.concatenate(
         [second[i : i + sources, cut:] for i in range(0, kept, sources)], axis=1
     )
-    sent_ref[...] = (
-        mm(slot_matrix(rows, kept, True), wide) + mm(spare_matrix(rows, True), spare)
-    ).astype(BF16)
+    both = jnp.concatenate([wide, spare], axis=0)
+    places = jnp.concatenate([slot_places(rows, kept), spare_places(rows)], axis=1)
+    size = rows // blocks
+    for block in range(blocks):
+        lines = slice(block * size, (block + 1) * size)
+        sent_ref[lines, :] = mm(
+            one_hot(size, places - block * size, True), both
+        ).astype(BF16)
+        leave(lines)
+
+
+def unpack_tail(sent, rest):
+    rows, lanes = sent.shape
+    places = spare_places(rows, (rows // SLOTS, 1))
+    spare = mm(one_hot(rows, places, False), sent).astype(BF16)
+    return jnp.concatenate([spare[:, i : i + rest] for i in range(0, lanes, rest)], axis=0)
 
 
 def unpack_rows(sent, kept, width):
     rows, lanes = sent.shape
-    sources = rows // SLOTS
-    rest = 2 * width - lanes
-    wide = mm(slot_matrix(rows, kept, False), sent).astype(BF16)
-    spare = mm(spare_matrix(rows, False), sent).astype(BF16)
-    tail = jnp.concatenate(
-        [spare[:, i * rest : (i + 1) * rest] for i in range(kept // sources)], axis=0
-    )
+    wide = mm(one_hot(rows, slot_places(rows, kept, (kept, 1)), False), sent).astype(BF16)
+    tail = unpack_tail(sent, 2 * width - lanes)
     return wide[:, :width], jnp.concatenate([wide[:, width:], tail], axis=1)
 
 
-def sums_kernel(
-    mine_ref, theirs_ref, own_ref, other_ref, sum_ref, kept_out, kept_ref, sem
-):
-    kept = sum_ref.shape[0]
+def part_sums(rows, half_ref):
+    width = half_ref.shape[0] // 3
+    for part, which in enumerate((0, 0, 1)):
+        yield part, mm(rows[which], half_ref[part * width : (part + 1) * width, :])
+
+
+def own_kernel(mine_ref, own_ref, sum_ref, kept_out, kept_ref, sem):
+    kept, wide = kept_ref.shape
     half = own_ref.shape[1]
     width = own_ref.shape[0] // 3
-    side = kept_ref.shape[1] // 2
     mine = unpack_rows(mine_ref[...], kept, width)
     kept_ref[...] = jnp.zeros_like(kept_ref)
     kept_ref[:, 0:width] = mine[0]
-    kept_ref[:, side : side + width] = mine[1]
+    kept_ref[:, wide // 2 : wide // 2 + width] = mine[1]
     copy = pltpu.make_async_copy(kept_ref, kept_out, sem)
     copy.start()
-    theirs = unpack_rows(theirs_ref[...], kept, width)
-    for part, which in enumerate((0, 0, 1)):
-        block = slice(part * width, (part + 1) * width)
-        sum_ref[:, part * half : (part + 1) * half] = (
-            mm(mine[which], own_ref[block, :]) + mm(theirs[which], other_ref[block, :])
-        ).astype(BF16)
+    for part, value in part_sums(mine, own_ref):
+        sum_ref[:, part * half : (part + 1) * half] = value
     copy.wait()
+
+
+def sums_kernel(theirs_ref, other_ref, part_ref, sum_ref):
+    half = other_ref.shape[1]
+    theirs = unpack_rows(theirs_ref[...], sum_ref.shape[0], other_ref.shape[0] // 3)
+    for part, value in part_sums(theirs, other_ref):
+        columns = slice(part * half, (part + 1) * half)
+        sum_ref[:, columns] = (part_ref[:, columns] + value).astype(BF16)
 
 
 def power_of_two(exponent):
@@ -200,8 +226,9 @@
 
 def products_kernel(
     all_ref, kept_ref, gate_ref, up_ref, down_ref,
-    send_ref, gate_sum_ref, up_sum_ref, down_sum_ref,
-    hid_ref, dgate_ref, dup_ref, rows_ref, sem,
+    send_out, gate_out, up_out, down_out,
+    hid_ref, dgate_ref, dup_ref, rows_ref, gate_sum_ref, up_sum_ref, down_sum_ref,
+    sems,
 ):
     kept, hidden = hid_ref.shape
     half = hidden // 2
@@ -217,19 +244,31 @@
                 all_ref[lines, part * half : (part + 1) * half].astype(F32)
                 * scale[:, part : part + 1]
             ).astype(BF16)
+    token_rows = kept_ref[:, 0:width]
+    grad_rows = kept_ref[:, side : side + width]
+    copies = []
+
+    def leave(ref, out):
+        copies.append(pltpu.make_async_copy(ref, out, sems.at[len(copies)]))
+        copies[-1].start()
+
+    def leave_rows(lines):
+        leave(rows_ref.at[lines, :], send_out.at[lines, :])
+
+    for ref, out, rows, values_ref in (
+        (gate_sum_ref, gate_out, token_rows, dgate_ref),
+        (up_sum_ref, up_out, token_rows, dup_ref),
+        (down_sum_ref, down_out, grad_rows, hid_ref),
+    ):
+        ref[...] = mm(rows, values_ref[...], TN).astype(BF16)
+        leave(ref, out)
     out_rows = mm(hid_ref[...], down_ref[...], NT).astype(BF16)
     back_rows = (
         mm(dgate_ref[...], gate_ref[...], NT) + mm(dup_ref[...], up_ref[...], NT)
     ).astype(BF16)
-    pack_rows(out_rows, back_rows, rows_ref)
-    copy = pltpu.make_async_copy(rows_ref, send_ref, sem)
-    copy.start()
-    token_rows = kept_ref[:, 0:width]
-    grad_rows = kept_ref[:, side : side + width]
-    gate_sum_ref[...] = mm(token_rows, dgate_ref[...], TN).astype(BF16)
-    up_sum_ref[...] = mm(token_rows, dup_ref[...], TN).astype(BF16)
-    down_sum_ref[...] = mm(grad_rows, hid_ref[...], TN).astype(BF16)
-    copy.wait()
+    pack_rows(out_rows, back_rows, rows_ref, 4, leave_rows)
+    for copy in copies:
+        copy.wait()
 
 
 def combine_kernel(back_ref, mark_ref, scale_ref, mixed_ref, token_grad_ref):
@@ -265,12 +304,12 @@
         [((rows, lanes), BF16), ((kept, 2 * count), BF16), ((kept, 2 * count), BF16)],
         *routed,
         far=(0, 1, 2),
-        far_in=True,
+        far_in=(0, 1, 2, 3),
         limit=60 * 1024 * 1024,
         scratch=[pltpu.VMEM(a.shape, a.dtype) for a in routed]
         + [pltpu.VMEM((rows, lanes), BF16)]
         + [pltpu.VMEM((kept, 2 * count), BF16)] * 2
-        + [pltpu.SemaphoreType.DMA((7,))],
+        + [pltpu.SemaphoreType.DMA((10,))],
     )
     mine = lax.all_to_all(
         send.reshape(experts, SLOTS, lanes), ("node", "local"), 0, 0, tiled=True
@@ -282,12 +321,13 @@
     other = lax.ppermute(give, "rep", swap)
     theirs = lax.ppermute(mine, "rep", swap)
     sums, kept_rows = call(
-        sums_kernel,
-        [((kept, 3 * half), BF16), ((kept, 2 * side), BF16)],
-        mine, theirs, own, other,
+        own_kernel,
+        [((kept, 3 * half), F32), ((kept, 2 * side), BF16)],
+        mine, own,
         far=(1,),
         scratch=[pltpu.VMEM((kept, 2 * side), BF16), pltpu.SemaphoreType.DMA(())],
     )
+    (sums,) = call(sums_kernel, [((kept, 3 * half), BF16)], theirs, other, sums)
     sums = lax.all_to_all(
         sums.reshape(chips, kept // chips, 3 * half),
         "rep", 0, 0, tiled=True, axis_index_groups=lines,
@@ -304,11 +344,12 @@
         products_kernel,
         [((rows, lanes), BF16), grads, grads, grads],
         whole, kept_rows, gate_mat, up_mat, down_mat,
-        far=(0,),
+        far=(0, 1, 2, 3),
         scratch=[
             matrix, matrix, matrix,
             pltpu.VMEM((rows, lanes), BF16),
-            pltpu.SemaphoreType.DMA(()),
+            *[pltpu.VMEM(*grads)] * 3,
+            pltpu.SemaphoreType.DMA((7,)),
         ],
     )
     back = lax.all_to_all(

time: 142 us -> 140 us (0.986)
    pallas_call x6 -> x7, Pallas kernels: 10.8 us -> 10.3 us  [call(): pl.pallas_call(kernel, out_shape=[jax.ShapeDtypeStruct(shape, dtype) for...]
  transfers between devices with their start and end apart: 3 -> 3, of which waited for: 2 -> 2; matrix products, arithmetic and copies ran while one was open for 0% -> 0% of each run, Pallas kernels for 0% -> 1%
where the time goes in v5:
time: 140 us
  blocking collectives  93.7 us (67%)
  starting transfers between devices  21.2 us (15%)
  Pallas kernels  10.3 us (7%)
  waiting for transfers between devices  9.2 us (7%)
  local copies, waits for them, and re-layouts  3.94 us (3%)
    all_to_all x1, blocking collectives, shards(): lax.all_to_all(sums.reshape(chips, kept // chips, 3 * half), 'rep', 0, 0,...  47.3 us
    all_gather x1, blocking collectives, shards(): whole = lax.all_gather(piece, 'rep', axis=0, tiled=True)  24.3 us
    all_to_all x1, blocking collectives, shards(): lax.all_to_all(send_back.reshape(experts, SLOTS, lanes), ('node', 'local'...  22.1 us
    all_to_all x1, starting transfers between devices, shards(): lax.all_to_all(send.reshape(experts, SLOTS, lanes), ('node', 'local'), 0,...  17.3 us
    pallas_call x7, Pallas kernels, call(): pl.pallas_call(kernel, out_shape=[jax.ShapeDtypeStruct(shape, dtype) for...  10.3 us
    all_to_all x1, waiting for transfers between devices, shards(): lax.all_to_all(send.reshape(experts, SLOTS, lanes), ('node', 'local'), 0,...  8.76 us
    unnamed x16, local copies, waits for them, and re-layouts  3.94 us
  transfers between devices with their start and end apart: 3, of which 2 were waited for; matrix products, arithmetic and copies ran while one was open for 0% of the time, Pallas kernels for 1%

profile of v5, /device:TPU:4, one launch (start us, length us, event | category | flops | bytes accessed | tf_op | source)
XLA Modules:
  0.0 139.5 jit_solution(2133812378283862133)
XLA Ops:
  0.6 2.5 %shard_map.110 = (bf16[512,384]{1,0:T(8,128)(2,1)}, bf16[384,128]{1,0:T(8,128)(2,1)}, bf16[384,128]{1,0:T(8,128)(2,1)}) custom-call(s32[4,64]{1,0:T(4,128)} %bitcast.30, bf16[4,64]{1,0:T(4,128)(2,1)} %bitcast.31, bf16[64,224]{1,0:T(8,128)(2,1)} %token_in.1, bf16[64,224]{1,0:T(8,128)(2,1)} %grad_in.1), custom_call_target="tpu_custom_call" | custom-call | tf_op jit(solution)/shard_map/pallas_call | solution.py:27
  3.1 17.3 %all-to-all-start = ((bf16[64,8,384]{2,1,0:T(8,128)(2,1)}), bf16[64,8,384]{2,1,0:T(8,128)(2,1)S(1)}, u32[]{:S(2)}, u32[]{:S(2)}) async-start(bf16[64,8,384]{2,1,0:T(8,128)(2,1)} %bitcast.29), calls=%async_computation | async-start | bytes 786432 | tf_op jit(solution)/shard_map/all_to_all | solution.py:314
  20.5 0.0 copy-start
  20.5 1.0 copy-done
  21.5 0.0 copy-start.2
  21.5 1.0 copy-done.2
  22.5 0.0 copy-start.4
  22.5 1.0 copy-done.4
  23.5 0.1 shard_map.111
  23.6 1.9 %collective-permute-start.1 = (bf16[672,512]{1,0:T(8,128)(2,1)S(1)}, bf16[672,512]{1,0:T(8,128)(2,1)S(1)}, u32[]{:S(2)}, u32[]{:S(2)}) collective-permute-start(bf16[672,512]{1,0:T(8,128)(2,1)S(1)} %get-tuple-element.19), channel_id=1, source_target_pairs={{0,64},{64,0},{128,192},{192,128},{256,320},{320,256},{384,448},{4... | collective-permute-start | bytes 2064392 | tf_op jit(solution)/shard_map/ppermute | solution.py:321
  25.5 8.8 %all-to-all-done = bf16[64,8,384]{2,1,0:T(8,128)(2,1)S(1)} async-done(((bf16[64,8,384]{2,1,0:T(8,128)(2,1)}), bf16[64,8,384]{2,1,0:T(8,128)(2,1)S(1)}, u32[]{:S(2)}, u32[]{:S(2)}) %all-to-all-start) | async-done | bytes 393248 | tf_op jit(solution)/shard_map/all_to_all | solution.py:314
  34.3 1.9 %collective-permute-start = (bf16[512,384]{1,0:T(8,128)(2,1)S(1)}, bf16[512,384]{1,0:T(8,128)(2,1)S(1)}, u32[]{:S(2)}, u32[]{:S(2)}) collective-permute-start(bf16[512,384]{1,0:T(8,128)(2,1)S(1)} %bitcast.25), channel_id=1, source_target_pairs={{0,64},{64,0},{128,192},{192,128},{256,320},{320,256},{384,448},{4... | collective-permute-start | bytes 1179656 | tf_op jit(solution)/shard_map/ppermute | solution.py:322
  36.2 1.2 shard_map.112
  37.5 0.0 collective-permute-done.1.other_ref
  37.5 0.4 collective-permute-done.theirs_ref
  37.9 0.8 shard_map.113
  38.8 47.3 %all_to_all.15.sum_ref = bf16[8,48,1536]{2,1,0:T(8,128)(2,1)S(1)} all-to-all(bf16[8,48,1536]{2,1,0:T(8,128)(2,1)S(1)} %bitcast.18), channel_id=1, replica_groups={{0,128,256,384,512,640,768,896},{64,192,320,448,576,704,832,960},{1,129..., dimensions={0} | all-to-all | bytes 2359296 | tf_op jit(solution)/shard_map/all_to_all | solution.py:331
  86.1 0.4 shard_map.114
  86.5 24.3 %all-gather.1 = f16[768,1664]{1,0:T(8,128)(2,1)S(1)} all-gather(f16[48,1664]{1,0:T(8,128)(2,1)S(1)} %convert_element_type.6), channel_id=1, replica_groups=mesh['rep'=16,'node'=8,'local'=8] {'rep'}, dimensions={0}, use_global_device_ids=true | all-gather | bytes 2715648 | tf_op jit(solution)/shard_map/all_gather | solution.py:339
  110.8 0.0 copy-start.1
  110.8 0.0 copy-start.3
  110.8 0.0 copy-start.5
  110.8 0.4 convert_element_type.7.all_ref
  111.2 0.6 copy-done.1
  111.8 0.1 copy-done.3
  111.9 0.1 copy-done.5
  112.0 0.0 copy-start.6
  112.1 0.0 copy-start.7
  112.1 3.9 %shard_map.115 = (bf16[512,384]{1,0:T(8,128)(2,1)S(1)}, bf16[224,1024]{1,0:T(8,128)(2,1)}, bf16[224,1024]{1,0:T(8,128)(2,1)}, bf16[224,1024]{1,0:T(8,128)(2,1)}) custom-call(bf16[768,1664]{1,0:T(8,128)(2,1)S(1)} %convert_element_type.7.all_ref, bf16[384,512]{1,0:T(8,128)(2,1)S(1)} %get-tuple-element.22.kept_ref, bf16[224,1024]{1,0:T(8,128)(2,1)S(1)} %bitcast.20, ...), custom_call_target="tpu_custom_call" | custom-call | tf_op jit(solution)/shard_map/pallas_call | solution.py:27
  116.0 22.1 %all_to_all.16 = bf16[64,8,384]{2,1,0:T(8,128)(2,1)S(1)} all-to-all(bf16[64,8,384]{2,1,0:T(8,128)(2,1)S(1)} %bitcast.28), channel_id=1, replica_groups=mesh['rep'=16,'node'=8,'local'=8] {'node','local'}, dimensions={0} | all-to-all | bytes 786432 | tf_op jit(solution)/shard_map/all_to_all | solution.py:355
  138.1 0.0 copy-done.6
  138.1 0.0 copy-done.7
  138.1 1.4 %shard_map.116 = (bf16[64,224]{1,0:T(8,128)(2,1)}, bf16[64,224]{1,0:T(8,128)(2,1)}) custom-call(bf16[512,384]{1,0:T(8,128)(2,1)S(1)} %bitcast.27, bf16[384,128]{1,0:T(8,128)(2,1)S(1)} %copy-done.6, bf16[384,128]{1,0:T(8,128)(2,1)S(1)} %copy-done.7), custom_call_target="tpu_custom_call" | custom-call | tf_op jit(solution)/shard_map/pallas_call | solution.py:27
  (1 shorter events, 0.0 us)
Async XLA Ops:
  3.1 31.2 %all-to-all-start = ((bf16[64,8,384]{2,1,0:T(8,128)(2,1)}), bf16[64,8,384]{2,1,0:T(8,128)(2,1)S(1)}, u32[]{:S(2)}, u32[]{:S(2)}) async-start(bf16[64,8,384]{2,1,0:T(8,128)(2,1)} %bitcast.29), calls=%async_computation | async-start | bytes 786432 | tf_op jit(solution)/shard_map/all_to_all | solution.py:314
  20.5 1.0 copy-start
  21.5 1.0 copy-start.2
  22.5 1.0 copy-start.4
  23.6 13.9 %collective-permute-start.1 = (bf16[672,512]{1,0:T(8,128)(2,1)S(1)}, bf16[672,512]{1,0:T(8,128)(2,1)S(1)}, u32[]{:S(2)}, u32[]{:S(2)}) collective-permute-start(bf16[672,512]{1,0:T(8,128)(2,1)S(1)} %get-tuple-element.19), channel_id=1, source_target_pairs={{0,64},{64,0},{128,192},{192,128},{256,320},{320,256},{384,448},{4... | collective-permute-start | bytes 2064392 | tf_op jit(solution)/shard_map/ppermute | solution.py:321
  34.3 3.6 %collective-permute-start = (bf16[512,384]{1,0:T(8,128)(2,1)S(1)}, bf16[512,384]{1,0:T(8,128)(2,1)S(1)}, u32[]{:S(2)}, u32[]{:S(2)}) collective-permute-start(bf16[512,384]{1,0:T(8,128)(2,1)S(1)} %bitcast.25), channel_id=1, source_target_pairs={{0,64},{64,0},{128,192},{192,128},{256,320},{320,256},{384,448},{4... | collective-permute-start | bytes 1179656 | tf_op jit(solution)/shard_map/ppermute | solution.py:322
  110.8 1.0 copy-start.1
  110.8 1.2 copy-start.3
  110.8 1.3 copy-start.5
  112.0 26.1 %copy-start.6 = (bf16[384,128]{1,0:T(8,128)(2,1)S(1)}, bf16[384,128]{1,0:T(8,128)(2,1)}, u32[]{:S(2)}) copy-start(bf16[384,128]{1,0:T(8,128)(2,1)} %get-tuple-element.24.mark_ref) | copy-start | bytes 294916
  112.1 26.1 %copy-start.7 = (bf16[384,128]{1,0:T(8,128)(2,1)S(1)}, bf16[384,128]{1,0:T(8,128)(2,1)}, u32[]{:S(2)}) copy-start(bf16[384,128]{1,0:T(8,128)(2,1)} %get-tuple-element.25.scale_ref) | copy-start | bytes 294916

commit v6 on v5

--- a/solution.py
+++ b/solution.py
@@ -34,13 +34,21 @@
     )(*args)
 
 
-def pack_kernel(core_ref, gate_ref, up_ref, down_ref, own_ref, send_ref):
+def pack_kernel(
+    core_ref, gate_ref, up_ref, down_ref, mark_ref, scale_ref,
+    own_ref, send_ref, mark_out, scale_out, tail_out,
+):
     width, hidden = gate_ref.shape
     half = hidden // 2
     for ref, which in ((own_ref, core_ref[0]), (send_ref, 1 - core_ref[0])):
         start = pl.multiple_of(which * half, half)
         for part, mat_ref in enumerate((gate_ref, up_ref, down_ref)):
             ref[part * width : (part + 1) * width, :] = mat_ref[:, pl.ds(start, half)]
+    kept, rows = mark_ref.shape[0], mark_out.shape[1]
+    pack = one_hot(rows, slot_places(rows, kept, (kept, 1)), False)
+    mark_out[...] = mm(mark_ref[...], pack, TN).astype(BF16)
+    scale_out[...] = mm(scale_ref[...], pack, TN).astype(BF16)
+    tail_out[...] = mark_ref[...].T
 
 
 def route_kernel(
@@ -201,6 +209,7 @@
 
 def hidden_kernel(sum_ref, out_ref):
     half = sum_ref.shape[2] // 3
+    block = out_ref.shape[0]
     total = lambda part: jnp.sum(
         sum_ref[:, :, part * half : (part + 1) * half].astype(F32), axis=0
     )
@@ -211,17 +220,20 @@
         back * up * (sig * (1.0 + gate * (1.0 - sig))),
         back * (gate * sig),
     )
-    lane = lax.broadcasted_iota(jnp.int32, (gate.shape[0], 128), 1)
+    lane = lax.broadcasted_iota(jnp.int32, (block, 128), 1)
     exponents = jnp.zeros(lane.shape, F32)
-    for part, value in enumerate(values):
-        value = value.astype(BF16).astype(F32)
-        peak = jnp.max(jnp.abs(value), axis=1, keepdims=True)
-        exponent = jnp.ceil(jnp.log2(jnp.maximum(peak, 2.0**-100))) - 15.0
-        out_ref[:, part * half : (part + 1) * half] = (
-            value * power_of_two(-exponent)
-        ).astype(out_ref.dtype)
-        exponents = jnp.where(lane == part, exponent, exponents)
-    out_ref[:, 3 * half :] = exponents.astype(out_ref.dtype)
+    place = 0
+    for row in range(0, gate.shape[0], block):
+        for value in values:
+            value = value[row : row + block].astype(BF16).astype(F32)
+            peak = jnp.max(jnp.abs(value), axis=1, keepdims=True)
+            exponent = jnp.ceil(jnp.log2(jnp.maximum(peak, 2.0**-100))) - 15.0
+            out_ref[:, place * half : (place + 1) * half] = (
+                value * power_of_two(-exponent)
+            ).astype(out_ref.dtype)
+            exponents = jnp.where(lane == place, exponent, exponents)
+            place += 1
+    out_ref[:, place * half :] = exponents.astype(out_ref.dtype)
 
 
 def products_kernel(
@@ -235,14 +247,17 @@
     width = gate_ref.shape[0]
     side = kept_ref.shape[1] // 2
     block = all_ref.shape[0] // 16
+    strips = kept // 8 // block
     for index in range(16):
         chip, core = index // 2, index % 2
         lines = slice(index * block, (index + 1) * block)
-        scale = power_of_two(all_ref[lines, 3 * half :].astype(F32))
-        for part, ref in enumerate((hid_ref, dgate_ref, dup_ref)):
-            ref[chip * block : (chip + 1) * block, core * half : (core + 1) * half] = (
-                all_ref[lines, part * half : (part + 1) * half].astype(F32)
-                * scale[:, part : part + 1]
+        scale = power_of_two(all_ref[lines, 3 * strips * half :].astype(F32))
+        for place in range(3 * strips):
+            ref = (hid_ref, dgate_ref, dup_ref)[place % 3]
+            row = (chip * strips + place // 3) * block
+            ref[row : row + block, core * half : (core + 1) * half] = (
+                all_ref[lines, place * half : (place + 1) * half].astype(F32)
+                * scale[:, place : place + 1]
             ).astype(BF16)
     token_rows = kept_ref[:, 0:width]
     grad_rows = kept_ref[:, side : side + width]
@@ -271,11 +286,20 @@
         copy.wait()
 
 
-def combine_kernel(back_ref, mark_ref, scale_ref, mixed_ref, token_grad_ref):
+def combine_kernel(back_ref, mark_ref, scale_ref, tail_ref, mixed_ref, token_grad_ref):
     tokens, width = mixed_ref.shape
-    back = unpack_rows(back_ref[...], mark_ref.shape[0], width)
-    for ref, marks, values in zip((mixed_ref, token_grad_ref), (scale_ref, mark_ref), back):
-        parts = mm(marks[...], values, TN).astype(BF16).astype(F32)
+    lanes = back_ref.shape[1]
+    tail = unpack_tail(back_ref[...], 2 * width - lanes)
+    for ref, parts in (
+        (mixed_ref, mm(scale_ref[...], back_ref[:, :width])),
+        (
+            token_grad_ref,
+            jnp.concatenate(
+                [mm(mark_ref[...], back_ref[:, width:]), mm(tail_ref[...], tail)], axis=1
+            ),
+        ),
+    ):
+        parts = parts.astype(BF16).astype(F32)
         ref[...] = (parts[0:tokens] + parts[tokens:]).astype(BF16)
 
 
@@ -315,8 +339,12 @@
         send.reshape(experts, SLOTS, lanes), ("node", "local"), 0, 0, tiled=True
     ).reshape(rows, lanes)
     packed = ((3 * width, half), BF16)
-    own, give = call(
-        pack_kernel, [packed, packed], core, gate_mat, up_mat, down_mat, scalars=1
+    marked = ((2 * count, rows), BF16)
+    own, give, mark, scale, tail = call(
+        pack_kernel,
+        [packed, packed, marked, marked, ((2 * count, kept), BF16)],
+        core, gate_mat, up_mat, down_mat, mark, scale,
+        scalars=1,
     )
     other = lax.ppermute(give, "rep", swap)
     theirs = lax.ppermute(mine, "rep", swap)
@@ -333,7 +361,7 @@
         "rep", 0, 0, tiled=True, axis_index_groups=lines,
     )
     (piece,) = call(
-        hidden_kernel, [((kept // chips, 3 * half + 128), BF16)], sums
+        hidden_kernel, [((16, kept // chips // 16 * 3 * half + 128), BF16)], sums
     )
     piece = lax.optimization_barrier(piece.astype(jnp.float16))
     whole = lax.all_gather(piece, "rep", axis=0, tiled=True)
@@ -358,7 +386,7 @@
     mixed, token_grad = call(
         combine_kernel,
         [(tokens.shape, BF16), (tokens.shape, BF16)],
-        back.reshape(rows, lanes), mark, scale,
+        back.reshape(rows, lanes), mark, scale, tail,
     )
     return (mixed, token_grad, gate_sum[None], up_sum[None], down_sum.T[None])
 

time: 140 us -> 139 us (level)
  waiting for transfers between devices: 9.2 us -> 7.06 us
  local copies, waits for them, and re-layouts: 3.94 us -> 5.85 us
    all_to_all x1, waiting for transfers between devices: 8.76 us -> 6.63 us  [shards(): lax.all_to_all(send.reshape(experts, SLOTS, lanes), ('node', 'local'), 0,...]
    unnamed x16, local copies, waits for them, and re-layouts: 3.94 us -> 5.85 us
where the time goes in v6:
time: 139 us; the launch traced here: 138 us
  blocking collectives  93 us (67%)
  starting transfers between devices  21.2 us (15%)
  Pallas kernels  10 us (7%)
  waiting for transfers between devices  7.06 us (5%)
  local copies, waits for them, and re-layouts  5.85 us (4%)
    all_to_all x1, blocking collectives, shards(): lax.all_to_all(sums.reshape(chips, kept // chips, 3 * half), 'rep', 0, 0,...  47.3 us
    all_gather x1, blocking collectives, shards(): whole = lax.all_gather(piece, 'rep', axis=0, tiled=True)  23.5 us
    all_to_all x1, blocking collectives, shards(): lax.all_to_all(send_back.reshape(experts, SLOTS, lanes), ('node', 'local'...  22.1 us
    all_to_all x1, starting transfers between devices, shards(): lax.all_to_all(send.reshape(experts, SLOTS, lanes), ('node', 'local'), 0,...  17.3 us
    pallas_call x7, Pallas kernels, call(): pl.pallas_call(kernel, out_shape=[jax.ShapeDtypeStruct(shape, dtype) for...  10 us
    all_to_all x1, waiting for transfers between devices, shards(): lax.all_to_all(send.reshape(experts, SLOTS, lanes), ('node', 'local'), 0,...  6.63 us
    unnamed x16, local copies, waits for them, and re-layouts  5.85 us
  transfers between devices with their start and end apart: 3, of which 2 were waited for; matrix products, arithmetic and copies ran while one was open for 0% of the time, Pallas kernels for 1%

profile of v6, /device:TPU:4, one launch (start us, length us, event | category | flops | bytes accessed | tf_op | source)
XLA Modules:
  0.0 138.1 jit_solution(9443810659639493479)
XLA Ops:
  0.6 2.5 %shard_map.110 = (bf16[512,384]{1,0:T(8,128)(2,1)}, bf16[384,128]{1,0:T(8,128)(2,1)}, bf16[384,128]{1,0:T(8,128)(2,1)}) custom-call(s32[4,64]{1,0:T(4,128)} %bitcast.30, bf16[4,64]{1,0:T(4,128)(2,1)} %bitcast.31, bf16[64,224]{1,0:T(8,128)(2,1)} %token_in.1, bf16[64,224]{1,0:T(8,128)(2,1)} %grad_in.1), custom_call_target="tpu_custom_call" | custom-call | tf_op jit(solution)/shard_map/pallas_call | solution.py:27
  3.1 17.3 %all-to-all-start = ((bf16[64,8,384]{2,1,0:T(8,128)(2,1)}), bf16[64,8,384]{2,1,0:T(8,128)(2,1)S(1)}, u32[]{:S(2)}, u32[]{:S(2)}) async-start(bf16[64,8,384]{2,1,0:T(8,128)(2,1)} %bitcast.29), calls=%async_computation | async-start | bytes 786432 | tf_op jit(solution)/shard_map/all_to_all | solution.py:338
  20.5 0.0 copy-start
  20.5 1.0 copy-done
  21.5 0.0 copy-start.2
  21.5 1.0 copy-done.2
  22.5 0.0 copy-start.4
  22.5 1.0 copy-done.4
  23.5 0.0 copy-start.6
  23.5 0.9 copy-done.6
  24.4 0.0 copy-start.7
  24.4 0.9 copy-done.7
  25.3 0.4 shard_map.111
  25.7 1.9 %collective-permute-start.1 = (bf16[672,512]{1,0:T(8,128)(2,1)S(1)}, bf16[672,512]{1,0:T(8,128)(2,1)S(1)}, u32[]{:S(2)}, u32[]{:S(2)}) collective-permute-start(bf16[672,512]{1,0:T(8,128)(2,1)S(1)} %get-tuple-element.24), channel_id=1, source_target_pairs={{0,64},{64,0},{128,192},{192,128},{256,320},{320,256},{384,448},{4... | collective-permute-start | bytes 2064392 | tf_op jit(solution)/shard_map/ppermute | solution.py:349
  27.7 6.6 %all-to-all-done = bf16[64,8,384]{2,1,0:T(8,128)(2,1)S(1)} async-done(((bf16[64,8,384]{2,1,0:T(8,128)(2,1)}), bf16[64,8,384]{2,1,0:T(8,128)(2,1)S(1)}, u32[]{:S(2)}, u32[]{:S(2)}) %all-to-all-start) | async-done | bytes 393248 | tf_op jit(solution)/shard_map/all_to_all | solution.py:338
  34.3 1.9 %collective-permute-start = (bf16[512,384]{1,0:T(8,128)(2,1)S(1)}, bf16[512,384]{1,0:T(8,128)(2,1)S(1)}, u32[]{:S(2)}, u32[]{:S(2)}) collective-permute-start(bf16[512,384]{1,0:T(8,128)(2,1)S(1)} %bitcast.25), channel_id=1, source_target_pairs={{0,64},{64,0},{128,192},{192,128},{256,320},{320,256},{384,448},{4... | collective-permute-start | bytes 1179656 | tf_op jit(solution)/shard_map/ppermute | solution.py:350
  36.2 1.2 shard_map.112
  37.5 0.0 collective-permute-done.1.other_ref
  37.5 0.4 collective-permute-done.theirs_ref
  37.9 0.8 shard_map.113
  38.8 47.3 %all_to_all.15.sum_ref = bf16[8,48,1536]{2,1,0:T(8,128)(2,1)S(1)} all-to-all(bf16[8,48,1536]{2,1,0:T(8,128)(2,1)S(1)} %bitcast.18), channel_id=1, replica_groups={{0,128,256,384,512,640,768,896},{64,192,320,448,576,704,832,960},{1,129..., dimensions={0} | all-to-all | bytes 2359296 | tf_op jit(solution)/shard_map/all_to_all | solution.py:359
  86.1 0.4 shard_map.114
  86.5 23.5 %all-gather.1 = f16[256,4736]{1,0:T(8,128)(2,1)S(1)} all-gather(f16[16,4736]{1,0:T(8,128)(2,1)S(1)} %convert_element_type.6), channel_id=1, replica_groups=mesh['rep'=16,'node'=8,'local'=8] {'rep'}, dimensions={0}, use_global_device_ids=true | all-gather | bytes 2576384 | tf_op jit(solution)/shard_map/all_gather | solution.py:367
  110.0 0.0 copy-start.1
  110.0 0.0 copy-start.3
  110.0 0.0 copy-start.5
  110.0 0.3 convert_element_type.7.all_ref
  110.3 0.7 copy-done.1
  111.1 0.1 copy-done.3
  111.2 0.1 copy-done.5
  111.3 3.6 %shard_map.115 = (bf16[512,384]{1,0:T(8,128)(2,1)S(1)}, bf16[224,1024]{1,0:T(8,128)(2,1)}, bf16[224,1024]{1,0:T(8,128)(2,1)}, bf16[224,1024]{1,0:T(8,128)(2,1)}) custom-call(bf16[256,4736]{1,0:T(8,128)(2,1)S(1)} %convert_element_type.7.all_ref, bf16[384,512]{1,0:T(8,128)(2,1)S(1)} %get-tuple-element.27.kept_ref, bf16[224,1024]{1,0:T(8,128)(2,1)S(1)} %bitcast.20, ...), custom_call_target="tpu_custom_call" | custom-call | tf_op jit(solution)/shard_map/pallas_call | solution.py:27
  114.9 22.1 %all_to_all.16 = bf16[64,8,384]{2,1,0:T(8,128)(2,1)S(1)} all-to-all(bf16[64,8,384]{2,1,0:T(8,128)(2,1)S(1)} %bitcast.28), channel_id=1, replica_groups=mesh['rep'=16,'node'=8,'local'=8] {'node','local'}, dimensions={0} | all-to-all | bytes 786432 | tf_op jit(solution)/shard_map/all_to_all | solution.py:383
  137.0 1.1 shard_map.116
  (1 shorter events, 0.0 us)
Async XLA Ops:
  3.1 31.2 %all-to-all-start = ((bf16[64,8,384]{2,1,0:T(8,128)(2,1)}), bf16[64,8,384]{2,1,0:T(8,128)(2,1)S(1)}, u32[]{:S(2)}, u32[]{:S(2)}) async-start(bf16[64,8,384]{2,1,0:T(8,128)(2,1)} %bitcast.29), calls=%async_computation | async-start | bytes 786432 | tf_op jit(solution)/shard_map/all_to_all | solution.py:338
  20.5 1.0 copy-start
  21.5 1.0 copy-start.2
  22.5 1.0 copy-start.4
  23.5 0.9 copy-start.6
  24.4 0.9 copy-start.7
  25.7 11.7 %collective-permute-start.1 = (bf16[672,512]{1,0:T(8,128)(2,1)S(1)}, bf16[672,512]{1,0:T(8,128)(2,1)S(1)}, u32[]{:S(2)}, u32[]{:S(2)}) collective-permute-start(bf16[672,512]{1,0:T(8,128)(2,1)S(1)} %get-tuple-element.24), channel_id=1, source_target_pairs={{0,64},{64,0},{128,192},{192,128},{256,320},{320,256},{384,448},{4... | collective-permute-start | bytes 2064392 | tf_op jit(solution)/shard_map/ppermute | solution.py:349
  34.3 3.6 %collective-permute-start = (bf16[512,384]{1,0:T(8,128)(2,1)S(1)}, bf16[512,384]{1,0:T(8,128)(2,1)S(1)}, u32[]{:S(2)}, u32[]{:S(2)}) collective-permute-start(bf16[512,384]{1,0:T(8,128)(2,1)S(1)} %bitcast.25), channel_id=1, source_target_pairs={{0,64},{64,0},{128,192},{192,128},{256,320},{320,256},{384,448},{4... | collective-permute-start | bytes 1179656 | tf_op jit(solution)/shard_map/ppermute | solution.py:350
  110.0 1.0 copy-start.1
  110.0 1.2 copy-start.3
  110.0 1.3 copy-start.5
